TPU v7x, 32 devices: a whole 2x2x4 slice. The times are simulated.
32 devices in a mesh: req: 16 (over z, x, core), tp: 2 (over y).
Axes of the slice: x: 2, y: 2, z: 4, core: 2. Of those that a mesh axis runs over, the one named last changes fastest.
Arguments:
- query: bfloat16 [1792, 3072], P('req', 'tp'), may hold values from -48 to 48
- key: bfloat16 [1792, 3072], P('req', 'tp'), may hold values from -12 to 12
- value: bfloat16 [1792, 3072], P('req', 'tp'), may hold values from -6 to 6
- cross_query: bfloat16 [1792, 3072], P('req', 'tp'), may hold values from -48 to 48
- text_key: bfloat16 [2048, 3072], P('req', 'tp'), may hold values from -12 to 12
- text_value: bfloat16 [2048, 3072], P('req', 'tp'), may hold values from -6 to 6
- wo_self: bfloat16 [3072, 5120], P('tp', 'req'), may hold values from -3 to 3
- wo_cross: bfloat16 [3072, 5120], P('tp', 'req'), may hold values from -3 to 3
- attn_gate: float32 [4, 5120], replicated, may hold values from 0.5 to 1.5
- mix_coef: float32 [5120], P('tp'), may hold values from 0.1 to 0.4
- latent: bfloat16 [1792, 5120], P('req', 'tp'), may hold values from -6 to 6
- tenant_len: int32 [4], replicated, may hold values from 1 to 448, as said below
- text_len: int32 [4], replicated, may hold values from 2 to 512, as said below
- t_index: int32 [4], replicated, may hold values from 0 to 49
Outputs:
- velocity: bfloat16 [1792, 5120], P('req', 'tp')
- updated: float32 [1792, 5120], P('req', 'tp')
Inputs may be any that keep to these rules, and one draw needn't show every extreme that they name: `tenant_len`: tenant t's latent tokens fill the slots of req indices t, t + 4, t + 8, ... in order from the first slot; one tenant fills all 448 slots. `text_len`: one tenant's prompt has all 512 tokens.
All inputs are finite; a program needn't handle non-finite values.
Results may differ from a plain program's by a relative error of at most 0.019.
Values may be sent and summed in bfloat16 or wider, within the bound.
A program may use at most 128 MiB of HBM per device.

v0:
```python
import jax
import jax.numpy as jnp
from jax import lax
from jax.sharding import PartitionSpec as P

DH = 128
TENANTS = 4
STEPS = 50


def passed_along(block, axis, distance):
    devices = range(lax.axis_size(axis))
    route = [((i - distance) % len(devices), i) for i in devices]
    return lax.ppermute(block, axis, route)


def shifted(block, axis, distance):
    devices = range(lax.axis_size(axis))
    route = [(i - distance, i) for i in devices if i - distance in devices]
    return lax.ppermute(block, axis, route)


def attend_block(state, q_heads, k_block, v_block, valid):
    top, denom, accum = state
    heads = q_heads.shape[1]
    k_heads = k_block.reshape(k_block.shape[0], heads, DH)
    v_heads = v_block.reshape(v_block.shape[0], heads, DH)
    scores = jnp.einsum("qhd,khd->hqk", q_heads, k_heads, preferred_element_type=jnp.float32) * (
        1.0 / DH**0.5
    )
    scores = jnp.where(valid[None, None, :], scores, -1e30)
    new_top = jnp.maximum(top, jnp.max(scores, axis=-1))
    weights = jnp.where(valid[None, None, :], jnp.exp(scores - new_top[..., None]), 0.0)
    factor = jnp.exp(top - new_top)
    denom = denom * factor + jnp.sum(weights, axis=-1)
    mixed = jnp.einsum(
        "hqk,khd->hqd", weights.astype(jnp.bfloat16), v_heads, preferred_element_type=jnp.float32
    )
    return (new_top, denom, accum * factor[..., None] + mixed)


def finish(state, tiles, feat):
    top, denom, accum = state
    out = accum / denom[..., None]
    return out.transpose(1, 0, 2).reshape(tiles, feat).astype(jnp.bfloat16)


def shards(
    query,
    key,
    value,
    cross_query,
    text_key,
    text_value,
    wo_self,
    wo_cross,
    attn_gate,
    mix_coef,
    latent,
    tenant_len,
    text_len,
    t_index,
):
    tiles, feat = query.shape
    text_rows = text_key.shape[0]
    heads = feat // DH
    group = lax.axis_size("req") // TENANTS
    place = lax.axis_index("req")
    tenant = place % TENANTS
    slot = place // TENANTS
    picker = jnp.arange(TENANTS) == tenant
    my_len = jnp.sum(jnp.where(picker, tenant_len, 0))
    my_text = jnp.sum(jnp.where(picker, text_len, 0))
    my_step = jnp.sum(jnp.where(picker, t_index, 0))
    gate_row = jnp.sum(jnp.where(picker[:, None], attn_gate, 0.0), axis=0)
    q_heads = query.reshape(tiles, heads, DH)
    cq_heads = cross_query.reshape(tiles, heads, DH)
    row_ids = jnp.arange(tiles, dtype=jnp.int32)

    def absorb(held, blocks, root):
        state, text_keys, text_values = held
        k_block, v_block, tk_block, tv_block = blocks
        valid = root * tiles + row_ids < my_len
        state = attend_block(state, q_heads, k_block, v_block, valid)
        text_keys = lax.dynamic_update_slice_in_dim(text_keys, tk_block, root * text_rows, 0)
        text_values = lax.dynamic_update_slice_in_dim(text_values, tv_block, root * text_rows, 0)
        return (state, text_keys, text_values)

    def fresh(count):
        return (
            jnp.full((heads, count), -1e30, jnp.float32),
            jnp.zeros((heads, count), jnp.float32),
            jnp.zeros((heads, count, DH), jnp.float32),
        )

    all_text = group * text_rows
    empty_text = jnp.zeros((all_text, feat), text_key.dtype)
    start_blocks = (key, value, text_key, text_value)
    held = absorb((fresh(tiles), empty_text, empty_text), start_blocks, slot)

    def turn_cycle(j, carry):
        blocks, kept = carry
        blocks = passed_along((blocks[0], blocks[1], blocks[2], blocks[3]), "req", TENANTS)
        return (blocks, absorb(kept, blocks, (slot - j) % group))

    _, held = lax.fori_loop(1, group, turn_cycle, (start_blocks, held))
    self_state, text_keys, text_values = held
    self_out = finish(self_state, tiles, feat)
    text_valid = jnp.arange(all_text, dtype=jnp.int32) < my_text
    cross_state = attend_block(fresh(tiles), cq_heads, text_keys, text_values, text_valid)
    cross_out = finish(cross_state, tiles, feat)
    self_cols = lax.all_gather(wo_self, "req", axis=1, tiled=True)
    cross_cols = lax.all_gather(wo_cross, "req", axis=1, tiled=True)
    block = gate_row[None, :] * jnp.dot(self_out, self_cols, preferred_element_type=jnp.float32)
    block = block + jnp.dot(cross_out, cross_cols, preferred_element_type=jnp.float32)
    summed = lax.psum_scatter(block.astype(jnp.bfloat16), "tp", scatter_dimension=1, tiled=True)
    valid_rows = slot * tiles + row_ids < my_len
    branch = jnp.where(valid_rows[:, None], summed, jnp.zeros((), jnp.bfloat16))
    before = shifted(branch[-1:], "req", TENANTS)
    after = shifted(branch[:1], "req", -TENANTS)
    extended = jnp.concatenate([before, branch, after], axis=0).astype(jnp.float32)
    branch32 = branch.astype(jnp.float32)
    vel = branch32 + mix_coef[None, :] * (extended[:-2] + extended[2:] - 2.0 * branch32)
    vel = jnp.where(valid_rows[:, None], vel, 0.0)
    frac = 1.0 - my_step.astype(jnp.float32) / STEPS
    sigma = 5.0 * frac / (1.0 + 4.0 * frac)
    updated = latent.astype(jnp.float32) + sigma * vel
    return (vel.astype(jnp.bfloat16), updated)


def solution(mesh):
    placed = (
        P("req", "tp"),
        P("req", "tp"),
        P("req", "tp"),
        P("req", "tp"),
        P("req", "tp"),
        P("req", "tp"),
        P("tp", "req"),
        P("tp", "req"),
        P(),
        P("tp"),
        P("req", "tp"),
        P(),
        P(),
        P(),
    )
    return jax.shard_map(
        shards,
        mesh=mesh,
        in_specs=placed,
        out_specs=(P("req", "tp"), P("req", "tp")),
        check_vma=False,
    )
```

profile of v0, /device:TPU:0, one launch (start us, length us, event | category | flops | bytes accessed | tf_op | source)
XLA Modules:
  0.0 385.0 jit_solution(11983474497460691215)
XLA Ops:
  7.2 1.0 copy.91
  8.2 1.0 copy.90
  9.3 0.7 all-gather.5.cloned.1.call-update
  10.4 0.9 copy.33
  11.3 0.9 copy.34
  12.4 0.6 select_reduce_fusion.3
  13.1 0.6 add_compare_fusion
  13.7 1.3 fusion.55
  15.2 1.2 broadcast_in_dim.155.clone.1
  16.4 0.8 constant_dynamic-update-slice_fusion.2
  17.4 1.8 convolution_add_fusion.2
  19.2 231.3 %while.32 = (s32[]{:T(128)}, bf16[112,1536]{0,1:T(8,128)(2,1)}, bf16[112,1536]{0,1:T(8,128)(2,1)}, bf16[128,1536]{1,0:T(8,128)(2,1)S(1)}, bf16[128,1536]{1,0:T(8...) while((s32[]{:T(128)}, bf16[112,1536]{0,1:T(8,128)(2,1)}, ...), condition=%wide.region_7.8_spmd.clone, body=%wide.region_4.7_spmd.clone.sunk | while | flops 78772080 | bytes 14722008 | solution.py:106
  19.2 3.1 collective-permute-start
  22.2 1.6 collective-permute-start.1
  23.8 1.6 collective-permute-start.2
  26.1 16.5 %collective-permute-done = bf16[112,1536]{0,1:T(8,128)(2,1)S(1)} collective-permute-done((bf16[112,1536]{0,1:T(8,128)(2,1)}, bf16[112,1536]{0,1:T(8,128)(2,1)S(1)}, u32[]{:S(2)}, u32[]{:S(2)}) %collective-permute-start) | collective-permute-done | bytes 344096 | tf_op jit(solution)/shard_map/while/body/eval_jaxpr/ppermute | solution.py:14
  43.2 0.7 copy.79
  43.9 15.5 %collective-permute-done.1 = bf16[112,1536]{0,1:T(8,128)(2,1)S(1)} collective-permute-done((bf16[112,1536]{0,1:T(8,128)(2,1)}, bf16[112,1536]{0,1:T(8,128)(2,1)S(1)}, u32[]{:S(2)}, u32[]{:S(2)}) %collective-permute-start.1) | collective-permute-done | bytes 344096 | tf_op jit(solution)/shard_map/while/body/eval_jaxpr/ppermute | solution.py:14
  59.4 0.7 copy.80
  60.2 0.6 convolution_add_fusion.4
  60.8 15.5 %collective-permute-done.2 = bf16[128,1536]{1,0:T(8,128)(2,1)S(1)} collective-permute-done((bf16[128,1536]{1,0:T(8,128)(2,1)S(1)}, bf16[128,1536]{1,0:T(8,128)(2,1)S(1)}, u32[]{:S(2)}, u32[]{:S(2)}) %collective-permute-start.2) | collective-permute-done | bytes 393248 | tf_op jit(solution)/shard_map/while/body/eval_jaxpr/ppermute | solution.py:14
  76.3 14.3 %collective-permute-done.3 = bf16[128,1536]{1,0:T(8,128)(2,1)S(1)} collective-permute-done((bf16[128,1536]{1,0:T(8,128)(2,1)S(1)}, bf16[128,1536]{1,0:T(8,128)(2,1)S(1)}, u32[]{:S(2)}, u32[]{:S(2)}) %collective-permute-start.3) | collective-permute-done | bytes 393248 | tf_op jit(solution)/shard_map/while/body/eval_jaxpr/ppermute | solution.py:14
  90.6 0.8 constant_dynamic-update-slice_fusion.6
  91.4 0.8 constant_dynamic-update-slice_fusion.7
  92.2 1.1 collective-permute-start.1
  93.3 1.7 collective-permute-start.2
  95.0 2.2 collective-permute-start.3
  97.7 16.8 %collective-permute-done = bf16[112,1536]{0,1:T(8,128)(2,1)S(1)} collective-permute-done((bf16[112,1536]{0,1:T(8,128)(2,1)}, bf16[112,1536]{0,1:T(8,128)(2,1)S(1)}, u32[]{:S(2)}, u32[]{:S(2)}) %collective-permute-start) | collective-permute-done | bytes 344096 | tf_op jit(solution)/shard_map/while/body/eval_jaxpr/ppermute | solution.py:14
  115.1 0.7 copy.79
  115.9 15.4 %collective-permute-done.1 = bf16[112,1536]{0,1:T(8,128)(2,1)S(1)} collective-permute-done((bf16[112,1536]{0,1:T(8,128)(2,1)}, bf16[112,1536]{0,1:T(8,128)(2,1)S(1)}, u32[]{:S(2)}, u32[]{:S(2)}) %collective-permute-start.1) | collective-permute-done | bytes 344096 | tf_op jit(solution)/shard_map/while/body/eval_jaxpr/ppermute | solution.py:14
  131.3 0.7 copy.80
  132.1 0.6 convolution_add_fusion.4
  132.7 15.5 %collective-permute-done.2 = bf16[128,1536]{1,0:T(8,128)(2,1)S(1)} collective-permute-done((bf16[128,1536]{1,0:T(8,128)(2,1)S(1)}, bf16[128,1536]{1,0:T(8,128)(2,1)S(1)}, u32[]{:S(2)}, u32[]{:S(2)}) %collective-permute-start.2) | collective-permute-done | bytes 393248 | tf_op jit(solution)/shard_map/while/body/eval_jaxpr/ppermute | solution.py:14
  148.2 15.3 %collective-permute-done.3 = bf16[128,1536]{1,0:T(8,128)(2,1)S(1)} collective-permute-done((bf16[128,1536]{1,0:T(8,128)(2,1)S(1)}, bf16[128,1536]{1,0:T(8,128)(2,1)S(1)}, u32[]{:S(2)}, u32[]{:S(2)}) %collective-permute-start.3) | collective-permute-done | bytes 393248 | tf_op jit(solution)/shard_map/while/body/eval_jaxpr/ppermute | solution.py:14
  163.6 0.8 constant_dynamic-update-slice_fusion.6
  164.4 0.8 constant_dynamic-update-slice_fusion.7
  165.1 26.9 %collective-permute-start = (bf16[112,1536]{0,1:T(8,128)(2,1)}, bf16[112,1536]{0,1:T(8,128)(2,1)S(1)}, u32[]{:S(2)}, u32[]{:S(2)}) collective-permute-start(bf16[112,1536]{0,1:T(8,128)(2,1)} %get-tuple-element.535), channel_id=1, source_target_pairs={{24,0},{26,2},{28,4},{30,6},{0,8},{2,10},{4,12},{6,14},{8,16},{10,... | collective-permute-start | bytes 1032200 | tf_op jit(solution)/shard_map/while/body/eval_jaxpr/ppermute | solution.py:14
  192.1 2.5 collective-permute-start.1
  194.6 1.6 collective-permute-start.2
  196.8 8.5 %collective-permute-done = bf16[112,1536]{0,1:T(8,128)(2,1)S(1)} collective-permute-done((bf16[112,1536]{0,1:T(8,128)(2,1)}, bf16[112,1536]{0,1:T(8,128)(2,1)S(1)}, u32[]{:S(2)}, u32[]{:S(2)}) %collective-permute-start) | collective-permute-done | bytes 344096 | tf_op jit(solution)/shard_map/while/body/eval_jaxpr/ppermute | solution.py:14
  205.9 0.7 copy.79
  206.7 11.6 %collective-permute-done.1 = bf16[112,1536]{0,1:T(8,128)(2,1)S(1)} collective-permute-done((bf16[112,1536]{0,1:T(8,128)(2,1)}, bf16[112,1536]{0,1:T(8,128)(2,1)S(1)}, u32[]{:S(2)}, u32[]{:S(2)}) %collective-permute-start.1) | collective-permute-done | bytes 344096 | tf_op jit(solution)/shard_map/while/body/eval_jaxpr/ppermute | solution.py:14
  218.2 0.7 copy.80
  219.0 0.6 convolution_add_fusion.4
  219.6 15.5 %collective-permute-done.2 = bf16[128,1536]{1,0:T(8,128)(2,1)S(1)} collective-permute-done((bf16[128,1536]{1,0:T(8,128)(2,1)S(1)}, bf16[128,1536]{1,0:T(8,128)(2,1)S(1)}, u32[]{:S(2)}, u32[]{:S(2)}) %collective-permute-start.2) | collective-permute-done | bytes 393248 | tf_op jit(solution)/shard_map/while/body/eval_jaxpr/ppermute | solution.py:14
  235.1 13.7 %collective-permute-done.3 = bf16[128,1536]{1,0:T(8,128)(2,1)S(1)} collective-permute-done((bf16[128,1536]{1,0:T(8,128)(2,1)S(1)}, bf16[128,1536]{1,0:T(8,128)(2,1)S(1)}, u32[]{:S(2)}, u32[]{:S(2)}) %collective-permute-start.3) | collective-permute-done | bytes 393248 | tf_op jit(solution)/shard_map/while/body/eval_jaxpr/ppermute | solution.py:14
  248.9 0.8 constant_dynamic-update-slice_fusion.6
  249.7 0.8 constant_dynamic-update-slice_fusion.7
  250.4 1.8 copy.37
  252.5 2.6 copy.41
  255.1 0.6 select_reduce_fusion.1
  255.7 0.6 iota_compare_fusion
  256.4 0.7 bitcast_reduce_fusion
  257.1 0.8 fusion.14
  258.5 1.2 fusion.37
  260.7 12.5 %convolution_multiply_fusion.1 = f32[112,5120]{1,0:T(8,128)S(1)} fusion(bf16[112,1536]{0,1:T(8,128)(2,1)S(1)} %bitcast.77, bf16[1536,5120]{0,1:T(8,128)(2,1)} %all-gather.3.cloned.1.call-done, f32[5120]{0:T(1024)S(1)} %select_reduce_fusion), kind=kOutput, calls=%fused_computation.17 | convolution fusion | flops 1762181120 | bytes 18386944 | tf_op jit(solution)/shard_map/dot_general | solution.py:114
  273.2 61.7 %all-gather.5.cloned.1.call-done = bf16[1536,5120]{0,1:T(8,128)(2,1)} async-done(((bf16[1536,320]{0,1:T(8,128)(2,1)}), bf16[1536,5120]{0,1:T(8,128)(2,1)}) %all-gather.5.cloned.1.call-update) | async-done | bytes 15728656 | tf_op jit(solution)/shard_map/all_gather | solution.py:113
  334.9 11.6 %fusion.11 = bf16[112,5120]{1,0:T(8,128)(2,1)} fusion(f32[112,5120]{1,0:T(8,128)S(1)} %convolution_multiply_fusion.1, bf16[112,1536]{0,1:T(8,128)(2,1)S(1)} %bitcast.76, bf16[1536,5120]{0,1:T(8,128)(2,1)} %all-gather.5.cloned.1.call-done), kind=kOutput, calls=%fused_computation.19 | convolution fusion | flops 1762754560 | bytes 19513344 | tf_op jit(solution)/shard_map/dot_general | solution.py:115
  346.5 19.7 %reduce-scatter.2.cloned.1.call-done = bf16[112,2560]{1,0:T(8,128)(2,1)} async-done(((bf16[112,5120]{1,0:T(8,128)(2,1)}), bf16[112,2560]{1,0:T(8,128)(2,1)}) %reduce-scatter.2.cloned.1.call-update) | async-done | bytes 573456 | tf_op jit(solution)/shard_map/reduce_scatter | solution.py:116
  366.2 1.2 broadcast_select_fusion
  367.5 3.4 collective-permute-start.4
  370.9 1.3 collective-permute-start.5
  372.9 3.6 collective-permute-done.5
  376.7 1.8 multiply_add_fusion.1
  (77 shorter events, 6.7 us)
Async XLA Ops:
  7.2 253.5 %all-gather.3.cloned.1.call-start = ((), (), s32[]{:S(2)}) async-start(), calls=%async_computation.1 | async-start | bytes 16711680 | tf_op jit(solution)/shard_map/all_gather | solution.py:112
  8.2 1.9 copy-start.4
  9.3 1.1 copy-start.5
  9.3 2.0 copy-start.6
  9.3 325.6 %all-gather.5.cloned.1.call-start = ((), (), s32[]{:S(2)}) async-start(), calls=%async_computation.2 | async-start | bytes 16711680 | tf_op jit(solution)/shard_map/all_gather | solution.py:113
  10.0 2.4 copy-start.12
  10.0 356.2 %reduce-scatter.2.cloned.1.call-start = ((), (), s32[]{:S(2)}) async-start(), calls=%async_computation.3 | async-start | bytes 1720320 | tf_op jit(solution)/shard_map/reduce_scatter | solution.py:116
  17.4 1.8 copy-start
  19.2 23.4 %collective-permute-start = (bf16[112,1536]{0,1:T(8,128)(2,1)}, bf16[112,1536]{0,1:T(8,128)(2,1)S(1)}, u32[]{:S(2)}, u32[]{:S(2)}) collective-permute-start(bf16[112,1536]{0,1:T(8,128)(2,1)} %get-tuple-element.535), channel_id=1, source_target_pairs={{24,0},{26,2},{28,4},{30,6},{0,8},{2,10},{4,12},{6,14},{8,16},{10,... | collective-permute-start | bytes 1032200 | tf_op jit(solution)/shard_map/while/body/eval_jaxpr/ppermute | solution.py:14
  22.2 37.2 %collective-permute-start.1 = (bf16[112,1536]{0,1:T(8,128)(2,1)}, bf16[112,1536]{0,1:T(8,128)(2,1)S(1)}, u32[]{:S(2)}, u32[]{:S(2)}) collective-permute-start(bf16[112,1536]{0,1:T(8,128)(2,1)} %get-tuple-element.536), channel_id=1, source_target_pairs={{24,0},{26,2},{28,4},{30,6},{0,8},{2,10},{4,12},{6,14},{8,16},{10,... | collective-permute-start | bytes 1032200 | tf_op jit(solution)/shard_map/while/body/eval_jaxpr/ppermute | solution.py:14
  23.8 52.4 %collective-permute-start.2 = (bf16[128,1536]{1,0:T(8,128)(2,1)S(1)}, bf16[128,1536]{1,0:T(8,128)(2,1)S(1)}, u32[]{:S(2)}, u32[]{:S(2)}) collective-permute-start(bf16[128,1536]{1,0:T(8,128)(2,1)S(1)} %get-tuple-element.537), channel_id=1, source_target_pairs={{24,0},{26,2},{28,4},{30,6},{0,8},{2,10},{4,12},{6,14},{8,16},{10,... | collective-permute-start | bytes 1179656 | tf_op jit(solution)/shard_map/while/body/eval_jaxpr/ppermute | solution.py:14
  25.4 65.2 %collective-permute-start.3 = (bf16[128,1536]{1,0:T(8,128)(2,1)S(1)}, bf16[128,1536]{1,0:T(8,128)(2,1)S(1)}, u32[]{:S(2)}, u32[]{:S(2)}) collective-permute-start(bf16[128,1536]{1,0:T(8,128)(2,1)S(1)} %get-tuple-element.538), channel_id=1, source_target_pairs={{24,0},{26,2},{28,4},{30,6},{0,8},{2,10},{4,12},{6,14},{8,16},{10,... | collective-permute-start | bytes 1179656 | tf_op jit(solution)/shard_map/while/body/eval_jaxpr/ppermute | solution.py:14
  92.2 22.3 %collective-permute-start = (bf16[112,1536]{0,1:T(8,128)(2,1)}, bf16[112,1536]{0,1:T(8,128)(2,1)S(1)}, u32[]{:S(2)}, u32[]{:S(2)}) collective-permute-start(bf16[112,1536]{0,1:T(8,128)(2,1)} %get-tuple-element.535), channel_id=1, source_target_pairs={{24,0},{26,2},{28,4},{30,6},{0,8},{2,10},{4,12},{6,14},{8,16},{10,... | collective-permute-start | bytes 1032200 | tf_op jit(solution)/shard_map/while/body/eval_jaxpr/ppermute | solution.py:14
  92.2 39.1 %collective-permute-start.1 = (bf16[112,1536]{0,1:T(8,128)(2,1)}, bf16[112,1536]{0,1:T(8,128)(2,1)S(1)}, u32[]{:S(2)}, u32[]{:S(2)}) collective-permute-start(bf16[112,1536]{0,1:T(8,128)(2,1)} %get-tuple-element.536), channel_id=1, source_target_pairs={{24,0},{26,2},{28,4},{30,6},{0,8},{2,10},{4,12},{6,14},{8,16},{10,... | collective-permute-start | bytes 1032200 | tf_op jit(solution)/shard_map/while/body/eval_jaxpr/ppermute | solution.py:14
  93.3 54.9 %collective-permute-start.2 = (bf16[128,1536]{1,0:T(8,128)(2,1)S(1)}, bf16[128,1536]{1,0:T(8,128)(2,1)S(1)}, u32[]{:S(2)}, u32[]{:S(2)}) collective-permute-start(bf16[128,1536]{1,0:T(8,128)(2,1)S(1)} %get-tuple-element.537), channel_id=1, source_target_pairs={{24,0},{26,2},{28,4},{30,6},{0,8},{2,10},{4,12},{6,14},{8,16},{10,... | collective-permute-start | bytes 1179656 | tf_op jit(solution)/shard_map/while/body/eval_jaxpr/ppermute | solution.py:14
  95.0 68.6 %collective-permute-start.3 = (bf16[128,1536]{1,0:T(8,128)(2,1)S(1)}, bf16[128,1536]{1,0:T(8,128)(2,1)S(1)}, u32[]{:S(2)}, u32[]{:S(2)}) collective-permute-start(bf16[128,1536]{1,0:T(8,128)(2,1)S(1)} %get-tuple-element.538), channel_id=1, source_target_pairs={{24,0},{26,2},{28,4},{30,6},{0,8},{2,10},{4,12},{6,14},{8,16},{10,... | collective-permute-start | bytes 1179656 | tf_op jit(solution)/shard_map/while/body/eval_jaxpr/ppermute | solution.py:14
  165.1 40.1 %collective-permute-start = (bf16[112,1536]{0,1:T(8,128)(2,1)}, bf16[112,1536]{0,1:T(8,128)(2,1)S(1)}, u32[]{:S(2)}, u32[]{:S(2)}) collective-permute-start(bf16[112,1536]{0,1:T(8,128)(2,1)} %get-tuple-element.535), channel_id=1, source_target_pairs={{24,0},{26,2},{28,4},{30,6},{0,8},{2,10},{4,12},{6,14},{8,16},{10,... | collective-permute-start | bytes 1032200 | tf_op jit(solution)/shard_map/while/body/eval_jaxpr/ppermute | solution.py:14
  192.1 26.2 %collective-permute-start.1 = (bf16[112,1536]{0,1:T(8,128)(2,1)}, bf16[112,1536]{0,1:T(8,128)(2,1)S(1)}, u32[]{:S(2)}, u32[]{:S(2)}) collective-permute-start(bf16[112,1536]{0,1:T(8,128)(2,1)} %get-tuple-element.536), channel_id=1, source_target_pairs={{24,0},{26,2},{28,4},{30,6},{0,8},{2,10},{4,12},{6,14},{8,16},{10,... | collective-permute-start | bytes 1032200 | tf_op jit(solution)/shard_map/while/body/eval_jaxpr/ppermute | solution.py:14
  194.6 40.5 %collective-permute-start.2 = (bf16[128,1536]{1,0:T(8,128)(2,1)S(1)}, bf16[128,1536]{1,0:T(8,128)(2,1)S(1)}, u32[]{:S(2)}, u32[]{:S(2)}) collective-permute-start(bf16[128,1536]{1,0:T(8,128)(2,1)S(1)} %get-tuple-element.537), channel_id=1, source_target_pairs={{24,0},{26,2},{28,4},{30,6},{0,8},{2,10},{4,12},{6,14},{8,16},{10,... | collective-permute-start | bytes 1179656 | tf_op jit(solution)/shard_map/while/body/eval_jaxpr/ppermute | solution.py:14
  196.2 52.7 %collective-permute-start.3 = (bf16[128,1536]{1,0:T(8,128)(2,1)S(1)}, bf16[128,1536]{1,0:T(8,128)(2,1)S(1)}, u32[]{:S(2)}, u32[]{:S(2)}) collective-permute-start(bf16[128,1536]{1,0:T(8,128)(2,1)S(1)} %get-tuple-element.538), channel_id=1, source_target_pairs={{24,0},{26,2},{28,4},{30,6},{0,8},{2,10},{4,12},{6,14},{8,16},{10,... | collective-permute-start | bytes 1179656 | tf_op jit(solution)/shard_map/while/body/eval_jaxpr/ppermute | solution.py:14
  250.4 1.8 copy-start.7
  252.4 2.6 copy-start.10
  252.4 2.6 copy-start.11
  257.1 1.4 copy-start.2
  259.7 0.9 copy-start.8
  346.5 30.1 %copy-start.3 = (bf16[112,2560]{1,0:T(8,128)(2,1)S(1)}, bf16[112,2560]{1,0:T(8,128)(2,1)}, u32[]{:S(2)}) copy-start(bf16[112,2560]{1,0:T(8,128)(2,1)} %param.26) | copy-start | bytes 1720324
  346.5 30.1 %copy-start.9 = (f32[2560]{0:T(1024)S(1)}, f32[2560]{0:T(1024)}, u32[]{:S(2)}) copy-start(f32[2560]{0:T(1024)} %param.25) | copy-start | bytes 30724
  366.2 10.4 %copy-start.1 = (bf16[112,2560]{1,0:T(8,128)(2,1)S(1)}, bf16[112,2560]{1,0:T(8,128)(2,1)}, u32[]{:S(2)}) copy-start(bf16[112,2560]{1,0:T(8,128)(2,1)} %reduce-scatter.2.cloned.1.call-done) | copy-start | bytes 1720324
  367.5 5.4 %collective-permute-start.4 = (bf16[1,2560]{1,0:T(2,128)(2,1)S(1)}, bf16[1,2560]{1,0:T(2,128)(2,1)S(1)}, u32[]{:S(2)}, u32[]{:S(2)}) collective-permute-start(bf16[1,2560]{1,0:T(2,128)(2,1)S(1)} %get-tuple-element.413), channel_id=1, source_target_pairs={{0,8},{2,10},{4,12},{6,14},{8,16},{10,18},{12,20},{14,22},{16,24},... | collective-permute-start | bytes 15368 | tf_op jit(solution)/shard_map/ppermute | solution.py:20
  370.9 5.6 %collective-permute-start.5 = (bf16[1,2560]{1,0:T(2,128)(2,1)S(1)}, bf16[1,2560]{1,0:T(2,128)(2,1)S(1)}, u32[]{:S(2)}, u32[]{:S(2)}) collective-permute-start(bf16[1,2560]{1,0:T(2,128)(2,1)S(1)} %get-tuple-element.414), channel_id=1, source_target_pairs={{8,0},{10,2},{12,4},{14,6},{16,8},{18,10},{20,12},{22,14},{24,16},... | collective-permute-start | bytes 15368 | tf_op jit(solution)/shard_map/ppermute | solution.py:20
Sparse Core Ops, SparseCore 0:
  10.3 185.2 all-gather.2
  197.8 137.0 all-gather.4
  346.6 19.5 reduce-scatter.1
where the time goes:
time: 386 us; the launch traced here: 385 us
  waiting for transfers between devices  260 us (67%)
  starting transfers between devices  47.1 us (12%)
  matrix products  32.1 us (8%)
  local copies, waits for them, and re-layouts  21.6 us (6%)
  between operations  14.8 us (4%)
  other arithmetic  9.34 us (2%)
    ppermute x12, waiting for transfers between devices, passed_along(): return lax.ppermute(block, axis, route)  174 us
    all_gather x1, waiting for transfers between devices, shards(): cross_cols = lax.all_gather(wo_cross, 'req', axis=1, tiled=True)  61.7 us
    ppermute x12, starting transfers between devices, passed_along(): return lax.ppermute(block, axis, route)  42.3 us
    reduce_scatter x1, waiting for transfers between devices, shards(): lax.psum_scatter(block.astype(jnp.bfloat16), 'tp', scatter_dimension=1, t...  19.7 us
    dot_general x1, matrix products, shards(): jnp.dot(self_out, self_cols, preferred_element_type=jnp.float32)  12.5 us
    dot_general x1, matrix products, shards(): jnp.dot(cross_out, cross_cols, preferred_element_type=jnp.float32)  11.6 us
  transfers between devices with their start and end apart: 17, of which 15 were waited for; matrix products, arithmetic and copies ran while one was open for 12% of the time, Pallas kernels for 0%

commit v1 on v0

--- a/solution.py
+++ b/solution.py
@@ -1,6 +1,10 @@
+import functools
+
 import jax
 import jax.numpy as jnp
 from jax import lax
+from jax.experimental import pallas as pl
+from jax.experimental.pallas import tpu as pltpu
 from jax.sharding import PartitionSpec as P
 
 DH = 128
@@ -128,6 +132,474 @@
     return (vel.astype(jnp.bfloat16), updated)
 
 
+MESH = pl.DeviceIdType.MESH
+
+
+def attend_head(q, k, v, count):
+    scores = lax.dot_general(
+        q, k, (((1,), (1,)), ((), ())), preferred_element_type=jnp.float32
+    ) * (1.0 / DH**0.5)
+    valid = lax.broadcasted_iota(jnp.int32, scores.shape, 1) < count
+    scores = jnp.where(valid, scores, -1e30)
+    top = jnp.max(scores, axis=-1, keepdims=True)
+    weights = jnp.where(valid, jnp.exp(scores - top), 0.0)
+    denom = jnp.sum(weights, axis=-1, keepdims=True)
+    mixed = jnp.dot(weights.astype(jnp.bfloat16), v, preferred_element_type=jnp.float32)
+    return (mixed / denom).astype(jnp.bfloat16)
+
+
+def fused_kernel(
+    group,
+    len_ref,
+    text_ref,
+    q_in,
+    k_in,
+    v_in,
+    cq_in,
+    tk_in,
+    tv_in,
+    ws_in,
+    wc_in,
+    gate_ref,
+    mix_ref,
+    out,
+    q_all,
+    k_all,
+    v_all,
+    cq_all,
+    tk_all,
+    tv_all,
+    so_all,
+    co_all,
+    ws_all,
+    wc_all,
+    mix_all,
+    term,
+    term_in,
+    vel,
+    in_send,
+    in_recv,
+    in_local,
+    w_send,
+    w_recv,
+    w_local,
+    mix_send,
+    mix_recv,
+    at_send,
+    at_recv,
+    term_send,
+    term_recv,
+    out_send,
+    out_recv,
+    out_local,
+):
+    place = lax.axis_index("req")
+    y = lax.axis_index("tp")
+    t = lax.rem(place, TENANTS)
+    z = place // TENANTS
+    half = group // 2
+    tiles = q_in.shape[0]
+    rows = tiles * group
+    heads_here = q_in.shape[1] // (DH * group)
+    sibling = t + 1 - 2 * lax.rem(t, 2)
+    across = lax.rem(t + 2, TENANTS)
+    other = 1 - y
+    y_out = z // half
+    my_len = len_ref[t]
+    my_text = text_ref[t]
+
+    def peer(k):
+        return lax.rem(z + k, group)
+
+    barrier = pltpu.get_barrier_semaphore()
+    friends = [(z * TENANTS + sibling, y), (z * TENANTS + across, y), (place, other)]
+    for k in range(1, group):
+        friends += [(peer(k) * TENANTS + t, y), (peer(k) * TENANTS + t, other)]
+    for friend in friends:
+        pl.semaphore_signal(barrier, inc=1, device_id=friend, device_id_type=MESH)
+
+    moved = [
+        (q_in, q_all),
+        (k_in, k_all),
+        (v_in, v_all),
+        (cq_in, cq_all),
+        (tk_in, tk_all),
+        (tv_in, tv_all),
+    ]
+
+    def own_copy(a):
+        src, dst = moved[a]
+        n = src.shape[0]
+        width = heads_here * DH
+        return pltpu.make_async_copy(
+            src.at[:, pl.ds(pl.multiple_of(z * width, DH), width)],
+            dst.at[pl.ds(pl.multiple_of(z * n, 16), n), :],
+            in_local.at[a],
+        )
+
+    def in_copy(a, h, k):
+        src, dst = moved[a]
+        n = src.shape[0]
+        to = peer(k)
+        return pltpu.make_async_remote_copy(
+            src_ref=src.at[:, pl.ds(pl.multiple_of((to * heads_here + h) * DH, DH), DH)],
+            dst_ref=dst.at[
+                pl.ds(pl.multiple_of(z * n, 16), n), pl.ds(pl.multiple_of(h * DH, DH), DH)
+            ],
+            send_sem=in_send.at[a, h, k - 1],
+            recv_sem=in_recv.at[a, h, k - 1],
+            device_id=(to * TENANTS + t, y),
+            device_id_type=MESH,
+        )
+
+    weights = [(ws_in, ws_all), (wc_in, wc_all)]
+
+    def w_own(i):
+        src, dst = weights[i]
+        return pltpu.make_async_copy(src, dst.at[t], w_local.at[i])
+
+    def w_copy(i, hop):
+        src, dst = weights[i]
+        if hop == 2:
+            src, block = dst.at[across], across
+        else:
+            block = t
+        target = across if hop == 0 else sibling
+        return pltpu.make_async_remote_copy(
+            src_ref=src,
+            dst_ref=dst.at[block],
+            send_sem=w_send.at[i, hop],
+            recv_sem=w_recv.at[i, hop],
+            device_id=(z * TENANTS + target, y),
+            device_id_type=MESH,
+        )
+
+    mix_copy = pltpu.make_async_remote_copy(
+        src_ref=mix_all.at[y],
+        dst_ref=mix_all.at[y],
+        send_sem=mix_send,
+        recv_sem=mix_recv,
+        device_id=(place, other),
+        device_id_type=MESH,
+    )
+
+    for a in range(6):
+        own_copy(a).start()
+    for i in range(2):
+        w_own(i).start()
+    mix_all[y] = mix_ref[...]
+    for ref, filled in ((k_all, rows), (v_all, rows), (tk_all, group * tk_in.shape[0]), (tv_all, group * tv_in.shape[0])):
+        if ref.shape[0] > filled:
+            ref[filled:, :] = jnp.zeros((ref.shape[0] - filled, ref.shape[1]), ref.dtype)
+
+    pl.semaphore_wait(barrier, len(friends))
+
+    def send_head(h, carry):
+        for a in range(6):
+            for k in range(1, group):
+                in_copy(a, h, k).start()
+        return carry
+
+    lax.fori_loop(0, heads_here, send_head, 0)
+    for i in range(2):
+        w_copy(i, 0).start()
+    for i in range(2):
+        w_copy(i, 1).start()
+    mix_copy.start()
+    for a in range(6):
+        own_copy(a).wait()
+
+    gathered = [so_all, co_all]
+
+    def at_copy(i, h, k):
+        column = pl.ds(pl.multiple_of((z * heads_here + h) * DH, DH), DH)
+        return pltpu.make_async_remote_copy(
+            src_ref=gathered[i].at[:, column],
+            dst_ref=gathered[i].at[:, column],
+            send_sem=at_send.at[i, h, k - 1],
+            recv_sem=at_recv.at[i, h, k - 1],
+            device_id=(peer(k) * TENANTS + t, y),
+            device_id_type=MESH,
+        )
+
+    def do_head(h, carry):
+        here = pl.ds(pl.multiple_of(h * DH, DH), DH)
+        column = pl.ds(pl.multiple_of((z * heads_here + h) * DH, DH), DH)
+        for i, (qr, kr, vr, count) in enumerate(
+            ((q_all, k_all, v_all, my_len), (cq_all, tk_all, tv_all, my_text))
+        ):
+            for a in range(3 * i, 3 * i + 3):
+                for k in range(1, group):
+                    in_copy(a, h, k).wait_recv()
+            gathered[i][:, column] = attend_head(qr[:, here], kr[:, here], vr[:, here], count)
+            for k in range(1, group):
+                at_copy(i, h, k).start()
+        return carry
+
+    lax.fori_loop(0, heads_here, do_head, 0)
+
+    for i in range(2):
+        w_copy(i, 0).wait_recv()
+        w_copy(i, 2).start()
+    for i in range(2):
+        w_own(i).wait()
+        w_copy(i, 1).wait_recv()
+    for i in range(2):
+        w_copy(i, 2).wait_recv()
+    mix_copy.wait_recv()
+
+    def wait_attended(h, carry):
+        for i in range(2):
+            for k in range(1, group):
+                at_copy(i, h, k).wait_recv()
+        return carry
+
+    lax.fori_loop(0, heads_here, wait_attended, 0)
+
+    def term_copy(j):
+        return pltpu.make_async_remote_copy(
+            src_ref=term.at[j],
+            dst_ref=term_in.at[j],
+            send_sem=term_send.at[j],
+            recv_sem=term_recv.at[j],
+            device_id=(place, other),
+            device_id_type=MESH,
+        )
+
+    def project(n, carry):
+        block = lax.rem(2 * other + n, TENANTS)
+        total = jnp.dot(so_all[...], ws_all[block], preferred_element_type=jnp.float32)
+        total = gate_ref[pl.ds(block, 1), :] * total
+        total = total + jnp.dot(co_all[...], wc_all[block], preferred_element_type=jnp.float32)
+        term[n] = total.astype(jnp.bfloat16)
+
+        @pl.when(n < 2)
+        def _():
+            term_copy(n).start()
+
+        return carry
+
+    lax.fori_loop(0, TENANTS, project, 0)
+
+    def out_block(j):
+        return lax.rem(z, half) * TENANTS + 2 * y + j
+
+    def out_copy(j, k):
+        to = peer(k)
+        return pltpu.make_async_remote_copy(
+            src_ref=vel.at[j, pl.ds(pl.multiple_of(to * tiles, 16), tiles), :],
+            dst_ref=out.at[out_block(j)],
+            send_sem=out_send.at[j, k],
+            recv_sem=out_recv.at[out_block(j)],
+            device_id=(to * TENANTS + t, y_out),
+            device_id_type=MESH,
+        )
+
+    def out_own(j):
+        return pltpu.make_async_copy(
+            vel.at[j, pl.ds(pl.multiple_of(z * tiles, 16), tiles), :],
+            out.at[out_block(j)],
+            out_local.at[j],
+        )
+
+    def smooth(j, carry):
+        term_copy(j).wait_recv()
+        total = term[2 + j].astype(jnp.float32) + term_in[j].astype(jnp.float32)
+        branch = total.astype(jnp.bfloat16).astype(jnp.float32)
+        index = lax.broadcasted_iota(jnp.int32, branch.shape, 0)
+        branch = jnp.where(index < my_len, branch, 0.0)
+        before = jnp.where(index == 0, 0.0, pltpu.roll(branch, 1, 0))
+        after = jnp.where(index == rows - 1, 0.0, pltpu.roll(branch, rows - 1, 0))
+        mix = mix_all[y_out, pl.ds(out_block(j), 1), :]
+        speed = branch + mix * (before + after - 2.0 * branch)
+        vel[j] = jnp.where(index < my_len, speed, 0.0).astype(jnp.bfloat16)
+        for k in range(1, group):
+            out_copy(j, k).start()
+
+        @pl.when(y_out == y)
+        def _():
+            out_own(j).start()
+
+        @pl.when(y_out != y)
+        def _():
+            out_copy(j, 0).start()
+
+        return carry
+
+    lax.fori_loop(0, 2, smooth, 0)
+
+    def drain_head(h, carry):
+        for k in range(1, group):
+            for a in range(6):
+                in_copy(a, h, k).wait_send()
+            for i in range(2):
+                at_copy(i, h, k).wait_send()
+        return carry
+
+    lax.fori_loop(0, heads_here, drain_head, 0)
+    for i in range(2):
+        for hop in range(3):
+            w_copy(i, hop).wait_send()
+    mix_copy.wait_send()
+
+    def drain_out(j, carry):
+        term_copy(j).wait_send()
+        for k in range(1, group):
+            out_copy(j, k).wait_send()
+
+        @pl.when(y_out == y)
+        def _():
+            out_own(j).wait()
+
+        @pl.when(y_out != y)
+        def _():
+            out_copy(j, 0).wait_send()
+
+        return carry
+
+    lax.fori_loop(0, 2, drain_out, 0)
+
+    def arrive(b, carry):
+        mine = jnp.logical_and(y_out == y, b // 2 == lax.rem(z, half) * 2 + y)
+
+        @pl.when(jnp.logical_not(mine))
+        def _():
+            pltpu.make_async_remote_copy(
+                src_ref=vel.at[0, pl.ds(0, tiles), :],
+                dst_ref=out.at[b],
+                send_sem=out_send.at[0, 0],
+                recv_sem=out_recv.at[b],
+                device_id=(place, other),
+                device_id_type=MESH,
+            ).wait_recv()
+
+        return carry
+
+    lax.fori_loop(0, out.shape[0], arrive, 0)
+
+
+def fits(query, text_key, wo_self):
+    group = lax.axis_size("req") // TENANTS
+    heads = query.shape[1] // DH
+    return (
+        lax.axis_size("tp") == 2
+        and group >= 2
+        and group % 2 == 0
+        and heads % group == 0
+        and query.shape[0] % 16 == 0
+        and text_key.shape[0] % 16 == 0
+        and wo_self.shape[0] == query.shape[1]
+    )
+
+
+def by_heads(
+    query,
+    key,
+    value,
+    cross_query,
+    text_key,
+    text_value,
+    wo_self,
+    wo_cross,
+    attn_gate,
+    mix_coef,
+    latent,
+    tenant_len,
+    text_len,
+    t_index,
+):
+    tiles, feat = query.shape
+    text_rows = text_key.shape[0]
+    blocks = lax.axis_size("req")
+    group = blocks // TENANTS
+    cols = wo_self.shape[1]
+    heads_here = feat // DH // group
+    width = heads_here * DH
+    rows = tiles * group
+    padded = -(-rows // 128) * 128
+    texts = -(-text_rows * group // 128) * 128
+    place = lax.axis_index("req")
+    tenant = place % TENANTS
+    slot = place // TENANTS
+    gate = lax.dynamic_slice(attn_gate, (tenant, slot * TENANTS * cols), (1, TENANTS * cols))
+    gate = gate.reshape(TENANTS, cols)
+    mix = mix_coef.reshape(blocks // 2, cols)
+    bf = jnp.bfloat16
+    dma = pltpu.SemaphoreType.DMA
+    any_spec = pl.BlockSpec(memory_space=pl.ANY)
+    smem = pl.BlockSpec(memory_space=pltpu.SMEM)
+    vmem = pl.BlockSpec(memory_space=pltpu.VMEM)
+    flops = 4 * rows * width * (padded + texts) + 4 * rows * feat * TENANTS * cols
+    moved = pl.pallas_call(
+        functools.partial(fused_kernel, group),
+        out_shape=jax.ShapeDtypeStruct((blocks // 2, tiles, cols), bf),
+        in_specs=[smem, smem] + [any_spec] * 8 + [vmem, vmem],
+        out_specs=any_spec,
+        scratch_shapes=[
+            pltpu.VMEM((rows, width), bf),
+            pltpu.VMEM((padded, width), bf),
+            pltpu.VMEM((padded, width), bf),
+            pltpu.VMEM((rows, width), bf),
+            pltpu.VMEM((texts, width), bf),
+            pltpu.VMEM((texts, width), bf),
+            pltpu.VMEM((rows, feat), bf),
+            pltpu.VMEM((rows, feat), bf),
+            pltpu.VMEM((TENANTS, feat, cols), bf),
+            pltpu.VMEM((TENANTS, feat, cols), bf),
+            pltpu.VMEM((2, blocks // 2, cols), jnp.float32),
+            pltpu.VMEM((TENANTS, rows, cols), bf),
+            pltpu.VMEM((2, rows, cols), bf),
+            pltpu.VMEM((2, rows, cols), bf),
+            dma((6, heads_here, group - 1)),
+            dma((6, heads_here, group - 1)),
+            dma((6,)),
+            dma((2, 3)),
+            dma((2, 3)),
+            dma((2,)),
+            dma,
+            dma,
+            dma((2, heads_here, group - 1)),
+            dma((2, heads_here, group - 1)),
+            dma((2,)),
+            dma((2,)),
+            dma((2, group)),
+            dma((blocks // 2,)),
+            dma((2,)),
+        ],
+        compiler_params=pltpu.CompilerParams(
+            collective_id=0, has_side_effects=True, vmem_limit_bytes=48 * 1024 * 1024
+        ),
+        cost_estimate=pl.CostEstimate(
+            flops=flops, bytes_accessed=16 * feat * cols, transcendentals=rows * heads_here * (padded + texts)
+        ),
+        name="attend_project",
+    )(
+        tenant_len,
+        text_len,
+        query,
+        key,
+        value,
+        cross_query,
+        text_key,
+        text_value,
+        wo_self,
+        wo_cross,
+        gate,
+        mix,
+    )
+    velocity = moved.transpose(1, 0, 2).reshape(tiles, blocks // 2 * cols)
+    step = jnp.sum(jnp.where(jnp.arange(TENANTS) == tenant, t_index, 0))
+    frac = 1.0 - step.astype(jnp.float32) / STEPS
+    sigma = 5.0 * frac / (1.0 + 4.0 * frac)
+    return (velocity, latent.astype(jnp.float32) + sigma * velocity.astype(jnp.float32))
+
+
+def either(*arrays):
+    if fits(arrays[0], arrays[4], arrays[6]):
+        return by_heads(*arrays)
+    return shards(*arrays)
+
+
 def solution(mesh):
     placed = (
         P("req", "tp"),
@@ -146,7 +618,7 @@
         P(),
     )
     return jax.shard_map(
-        shards,
+        either,
         mesh=mesh,
         in_specs=placed,
         out_specs=(P("req", "tp"), P("req", "tp")),

time: 386 us -> 156 us (0.40)
  waiting for transfers between devices: 260 us -> 0 us
  Pallas kernels: 0 us -> 141 us
  starting transfers between devices: 47.1 us -> 0 us
  matrix products: 32.1 us -> 0 us
  between operations: 14.8 us -> 1.51 us
  local copies, waits for them, and re-layouts: 21.6 us -> 9.33 us
  other arithmetic: 9.34 us -> 2.48 us
    ppermute x14 -> x0, waiting for transfers between devices: 178 us -> none  [the longest x12 174 us: passed_along(): return lax.ppermute(block, axis, route)]
    pallas_call x0 -> x1, Pallas kernels: none -> 141 us  [by_heads(): pl.pallas_call(functools.partial(fused_kernel, group), out_shape=jax.Shap...]
    all_gather x2 -> x0, waiting for transfers between devices: 61.7 us -> none  [the longest x1 61.7 us: shards(): cross_cols = lax.all_gather(wo_cross, 'req', axis=1, tiled=True)]
    ppermute x14 -> x0, starting transfers between devices: 47 us -> none  [the longest x12 42.3 us: passed_along(): return lax.ppermute(block, axis, route)]
    dot_general x12 -> x0, matrix products: 32.1 us -> none  [the longest x1 12.5 us: shards(): jnp.dot(self_out, self_cols, preferred_element_type=jnp.float32)]
    reduce_scatter x1 -> x0, waiting for transfers between devices: 19.7 us -> none  [shards(): lax.psum_scatter(block.astype(jnp.bfloat16), 'tp', scatter_dimension=1, t...]
    while x17 -> x0, local copies, waits for them, and re-layouts: 9.01 us -> none
    dynamic_update_slice x8 -> x0, local copies, waits for them, and re-layouts: 5.51 us -> none  [the longest x4 3.11 us: absorb(): lax.dynamic_update_slice_in_dim(text_values, tv_block, root * text_rows, 0)]
  transfers between devices with their start and end apart: 17 -> 0, of which waited for: 15 -> 0; matrix products, arithmetic and copies ran while one was open for 12% -> 0% of each run, Pallas kernels for 0% -> 0%
where the time goes in v1:
time: 156 us; the launch traced here: 155 us
  Pallas kernels  141 us (90%)
  local copies, waits for them, and re-layouts  9.33 us (6%)
  other arithmetic  2.48 us (2%)
    pallas_call x1, Pallas kernels, by_heads(): pl.pallas_call(functools.partial(fused_kernel, group), out_shape=jax.Shap...  141 us
    unnamed x24, local copies, waits for them, and re-layouts  7.81 us

profile of v1, /device:TPU:0, one launch (start us, length us, event | category | flops | bytes accessed | tf_op | source)
XLA Modules:
  0.0 154.6 jit_solution(16172087936432324069)
XLA Ops:
  0.6 0.0 copy-start
  0.7 1.3 fusion
  2.7 0.0 copy-done
  2.7 0.1 dynamic-slice_reduce_fusion
  2.8 0.1 reshape.13.gate_ref
  2.9 0.8 reshape.14.mix_ref
  3.6 1.7 %copy.18.ws_in = bf16[1536,320]{1,0:T(8,128)(2,1)S(1)} copy(bf16[1536,320]{0,1:T(8,128)(2,1)} %param.20) | data formatting | bytes 1966080 | tf_op args[6]
  5.3 0.0 copy-start.1
  5.3 0.0 copy-start.2
  5.3 0.0 copy-start.7
  5.3 0.0 copy-start.8
  5.4 1.7 %copy.19.wc_in = bf16[1536,320]{1,0:T(8,128)(2,1)S(1)} copy(bf16[1536,320]{0,1:T(8,128)(2,1)} %param.21) | data formatting | bytes 1966080 | tf_op args[7]
  7.1 0.0 copy-done.1
  7.1 0.0 copy-done.2
  7.1 0.0 copy-done.7
  7.1 0.0 copy-done.8
  7.1 0.0 copy-start.3
  7.2 1.0 copy-done.3
  8.1 0.0 copy-start.4
  8.1 1.0 copy-done.4
  9.1 0.0 copy-start.5
  9.1 1.0 copy-done.5
  10.1 0.0 copy-start.6
  10.1 1.0 copy-done.6
  11.1 141.3 %attend_project.1 = bf16[8,112,320]{2,1,0:T(8,128)(2,1)S(1)} custom-call(s32[4]{0:T(128)S(1)} %copy-done.7, s32[4]{0:T(128)S(1)} %copy-done.8, bf16[112,1536]{1,0:T(8,128)(2,1)S(1)} %copy-done.3, bf16[112,1536]{1,0:T(8,128)(2,1)S(1)} %copy-done.4, bf16[112,1536]{1,0:T(8,128)(2,1)S(1)} %copy-done.5, bf16[112,1536]{1,0:T(8,128)(2,1)S(1)} %copy-done.6, ...), custom_call_target="tpu_custom_call" | custom-call | flops 4227858432 | bytes 7864320 | tf_op jit(solution)/shard_map/attend_project/pallas_call | solution.py:533
  152.3 0.0 copy-start.10
  152.3 0.1 copy.20
  152.5 0.4 reshape.15
  152.9 0.5 copy-done.10
  153.4 0.0 copy-start.9
  153.4 1.2 multiply_add_fusion
  154.6 0.0 copy-done.9
Async XLA Ops:
  0.6 2.0 %copy-start = (f32[4,5120]{1,0:T(4,128)S(1)}, f32[4,5120]{1,0:T(4,128)}, u32[]{:S(2)}) copy-start(f32[4,5120]{1,0:T(4,128)} %param.22) | copy-start | bytes 245764
  5.3 1.8 %copy-start.1 = (bf16[128,1536]{1,0:T(8,128)(2,1)S(1)}, bf16[128,1536]{1,0:T(8,128)(2,1)}, u32[]{:S(2)}) copy-start(bf16[128,1536]{1,0:T(8,128)(2,1)} %tk_in.1) | copy-start | bytes 1179652
  5.3 1.8 %copy-start.2 = (bf16[128,1536]{1,0:T(8,128)(2,1)S(1)}, bf16[128,1536]{1,0:T(8,128)(2,1)}, u32[]{:S(2)}) copy-start(bf16[128,1536]{1,0:T(8,128)(2,1)} %tv_in.1) | copy-start | bytes 1179652
  5.3 1.8 %copy-start.7 = (s32[4]{0:T(128)S(1)}, s32[4]{0:T(128)}, u32[]{:S(2)}) copy-start(s32[4]{0:T(128)} %len_ref.1) | copy-start | bytes 52
  5.3 1.8 %copy-start.8 = (s32[4]{0:T(128)S(1)}, s32[4]{0:T(128)}, u32[]{:S(2)}) copy-start(s32[4]{0:T(128)} %text_ref.1) | copy-start | bytes 52
  7.1 1.0 copy-start.3
  8.1 1.0 copy-start.4
  9.1 1.0 copy-start.5
  10.1 1.0 copy-start.6
  152.3 1.1 copy-start.10
  153.4 1.2 copy-start.9

commit v2 on v1

--- a/solution.py
+++ b/solution.py
@@ -175,6 +175,7 @@
     wc_all,
     mix_all,
     term,
+    term_own,
     term_in,
     vel,
     in_send,
@@ -254,20 +255,25 @@
 
     weights = [(ws_in, ws_all), (wc_in, wc_all)]
 
+    cols = ws_in.shape[0]
+
+    def w_rows(block):
+        return pl.ds(pl.multiple_of(block * cols, 16), cols)
+
     def w_own(i):
         src, dst = weights[i]
-        return pltpu.make_async_copy(src, dst.at[t], w_local.at[i])
+        return pltpu.make_async_copy(src, dst.at[w_rows(t), :], w_local.at[i])
 
     def w_copy(i, hop):
         src, dst = weights[i]
         if hop == 2:
-            src, block = dst.at[across], across
+            src, block = dst.at[w_rows(across), :], across
         else:
             block = t
         target = across if hop == 0 else sibling
         return pltpu.make_async_remote_copy(
             src_ref=src,
-            dst_ref=dst.at[block],
+            dst_ref=dst.at[w_rows(block), :],
             send_sem=w_send.at[i, hop],
             recv_sem=w_recv.at[i, hop],
             device_id=(z * TENANTS + target, y),
@@ -294,13 +300,13 @@
 
     pl.semaphore_wait(barrier, len(friends))
 
-    def send_head(h, carry):
-        for a in range(6):
-            for k in range(1, group):
+    def send_half(h, i):
+        for a in range(3 * i, 3 * i + 3):
+            for k in range(group - 1, 0, -1):
                 in_copy(a, h, k).start()
-        return carry
-
-    lax.fori_loop(0, heads_here, send_head, 0)
+
+    send_half(0, 0)
+    send_half(0, 1)
     for i in range(2):
         w_copy(i, 0).start()
     for i in range(2):
@@ -331,6 +337,11 @@
             for a in range(3 * i, 3 * i + 3):
                 for k in range(1, group):
                     in_copy(a, h, k).wait_recv()
+
+            @pl.when(h + 1 < heads_here)
+            def _():
+                send_half(h + 1, i)
+
             gathered[i][:, column] = attend_head(qr[:, here], kr[:, here], vr[:, here], count)
             for k in range(1, group):
                 at_copy(i, h, k).start()
@@ -356,64 +367,81 @@
 
     lax.fori_loop(0, heads_here, wait_attended, 0)
 
+    side = term.shape[1]
+    chunks = [(at, min(256, side - at)) for at in range(0, side, 256)]
+
     def term_copy(j):
+        at, n = chunks[j]
         return pltpu.make_async_remote_copy(
-            src_ref=term.at[j],
-            dst_ref=term_in.at[j],
+            src_ref=term.at[:, pl.ds(at, n)],
+            dst_ref=term_in.at[:, pl.ds(at, n)],
             send_sem=term_send.at[j],
             recv_sem=term_recv.at[j],
             device_id=(place, other),
             device_id_type=MESH,
         )
 
-    def project(n, carry):
-        block = lax.rem(2 * other + n, TENANTS)
-        total = jnp.dot(so_all[...], ws_all[block], preferred_element_type=jnp.float32)
-        total = gate_ref[pl.ds(block, 1), :] * total
-        total = total + jnp.dot(co_all[...], wc_all[block], preferred_element_type=jnp.float32)
-        term[n] = total.astype(jnp.bfloat16)
-
-        @pl.when(n < 2)
-        def _():
-            term_copy(n).start()
-
-        return carry
-
-    lax.fori_loop(0, TENANTS, project, 0)
-
-    def out_block(j):
-        return lax.rem(z, half) * TENANTS + 2 * y + j
+    def project(whose, j):
+        at, n = chunks[j]
+        start = pl.multiple_of(whose * side + at, 128)
+        across_rows = (((1,), (1,)), ((), ()))
+        total = lax.dot_general(
+            so_all[...], ws_all[pl.ds(start, n), :], across_rows, preferred_element_type=jnp.float32
+        )
+        first = pl.multiple_of(z * (2 * side) + whose * side + at, 128)
+        gates = gate_ref[:, pl.ds(first, n)]
+        mine = lax.broadcasted_iota(jnp.int32, gates.shape, 0) == t
+        total = jnp.sum(jnp.where(mine, gates, 0.0), axis=0, keepdims=True) * total
+        total = total + lax.dot_general(
+            co_all[...], wc_all[pl.ds(start, n), :], across_rows, preferred_element_type=jnp.float32
+        )
+        return total.astype(jnp.bfloat16)
+
+    for j, (at, n) in enumerate(chunks):
+        term[:, at : at + n] = project(other, j)
+        term_copy(j).start()
+    for j, (at, n) in enumerate(chunks):
+        term_own[:, at : at + n] = project(y, j)
+
+    source = lax.rem(z, half) * 2 + y
+
+    def out_columns(sender, j):
+        at, n = chunks[j]
+        return pl.ds(pl.multiple_of(sender * side + at, 128), n)
+
+    def vel_part(j, to):
+        at, n = chunks[j]
+        return vel.at[pl.ds(pl.multiple_of(to * tiles, 16), tiles), pl.ds(at, n)]
 
     def out_copy(j, k):
         to = peer(k)
         return pltpu.make_async_remote_copy(
-            src_ref=vel.at[j, pl.ds(pl.multiple_of(to * tiles, 16), tiles), :],
-            dst_ref=out.at[out_block(j)],
+            src_ref=vel_part(j, to),
+            dst_ref=out.at[:, out_columns(source, j)],
             send_sem=out_send.at[j, k],
-            recv_sem=out_recv.at[out_block(j)],
+            recv_sem=out_recv.at[source, j],
             device_id=(to * TENANTS + t, y_out),
             device_id_type=MESH,
         )
 
     def out_own(j):
         return pltpu.make_async_copy(
-            vel.at[j, pl.ds(pl.multiple_of(z * tiles, 16), tiles), :],
-            out.at[out_block(j)],
-            out_local.at[j],
-        )
-
-    def smooth(j, carry):
+            vel_part(j, z), out.at[:, out_columns(source, j)], out_local.at[j]
+        )
+
+    for j, (at, n) in enumerate(chunks):
         term_copy(j).wait_recv()
-        total = term[2 + j].astype(jnp.float32) + term_in[j].astype(jnp.float32)
+        total = term_own[:, at : at + n].astype(jnp.float32)
+        total = total + term_in[:, at : at + n].astype(jnp.float32)
         branch = total.astype(jnp.bfloat16).astype(jnp.float32)
         index = lax.broadcasted_iota(jnp.int32, branch.shape, 0)
         branch = jnp.where(index < my_len, branch, 0.0)
         before = jnp.where(index == 0, 0.0, pltpu.roll(branch, 1, 0))
         after = jnp.where(index == rows - 1, 0.0, pltpu.roll(branch, rows - 1, 0))
-        mix = mix_all[y_out, pl.ds(out_block(j), 1), :]
+        mix = mix_all[y_out, :, out_columns(source, j)]
         speed = branch + mix * (before + after - 2.0 * branch)
-        vel[j] = jnp.where(index < my_len, speed, 0.0).astype(jnp.bfloat16)
-        for k in range(1, group):
+        vel[:, at : at + n] = jnp.where(index < my_len, speed, 0.0).astype(jnp.bfloat16)
+        for k in range(group - 1, 0, -1):
             out_copy(j, k).start()
 
         @pl.when(y_out == y)
@@ -423,10 +451,6 @@
         @pl.when(y_out != y)
         def _():
             out_copy(j, 0).start()
-
-        return carry
-
-    lax.fori_loop(0, 2, smooth, 0)
 
     def drain_head(h, carry):
         for k in range(1, group):
@@ -442,7 +466,7 @@
             w_copy(i, hop).wait_send()
     mix_copy.wait_send()
 
-    def drain_out(j, carry):
+    for j in range(len(chunks)):
         term_copy(j).wait_send()
         for k in range(1, group):
             out_copy(j, k).wait_send()
@@ -455,27 +479,24 @@
         def _():
             out_copy(j, 0).wait_send()
 
-        return carry
-
-    lax.fori_loop(0, 2, drain_out, 0)
-
-    def arrive(b, carry):
-        mine = jnp.logical_and(y_out == y, b // 2 == lax.rem(z, half) * 2 + y)
+    def arrive(sender, carry):
+        mine = jnp.logical_and(y_out == y, sender == source)
 
         @pl.when(jnp.logical_not(mine))
         def _():
-            pltpu.make_async_remote_copy(
-                src_ref=vel.at[0, pl.ds(0, tiles), :],
-                dst_ref=out.at[b],
-                send_sem=out_send.at[0, 0],
-                recv_sem=out_recv.at[b],
-                device_id=(place, other),
-                device_id_type=MESH,
-            ).wait_recv()
+            for j in range(len(chunks)):
+                pltpu.make_async_remote_copy(
+                    src_ref=vel_part(j, 0),
+                    dst_ref=out.at[:, out_columns(sender, j)],
+                    send_sem=out_send.at[j, 0],
+                    recv_sem=out_recv.at[sender, j],
+                    device_id=(place, other),
+                    device_id_type=MESH,
+                ).wait_recv()
 
         return carry
 
-    lax.fori_loop(0, out.shape[0], arrive, 0)
+    lax.fori_loop(0, group, arrive, 0)
 
 
 def fits(query, text_key, wo_self):
@@ -489,6 +510,7 @@
         and query.shape[0] % 16 == 0
         and text_key.shape[0] % 16 == 0
         and wo_self.shape[0] == query.shape[1]
+        and wo_self.shape[1] % 64 == 0
     )
 
 
@@ -521,18 +543,18 @@
     place = lax.axis_index("req")
     tenant = place % TENANTS
     slot = place // TENANTS
-    gate = lax.dynamic_slice(attn_gate, (tenant, slot * TENANTS * cols), (1, TENANTS * cols))
-    gate = gate.reshape(TENANTS, cols)
-    mix = mix_coef.reshape(blocks // 2, cols)
+    side = cols * TENANTS // 2
+    chunks = -(-side // 256)
+    mix = mix_coef.reshape(1, -1)
     bf = jnp.bfloat16
     dma = pltpu.SemaphoreType.DMA
-    any_spec = pl.BlockSpec(memory_space=pl.ANY)
+    any_spec = pl.BlockSpec(memory_space=pltpu.HBM)
     smem = pl.BlockSpec(memory_space=pltpu.SMEM)
     vmem = pl.BlockSpec(memory_space=pltpu.VMEM)
     flops = 4 * rows * width * (padded + texts) + 4 * rows * feat * TENANTS * cols
-    moved = pl.pallas_call(
+    velocity = pl.pallas_call(
         functools.partial(fused_kernel, group),
-        out_shape=jax.ShapeDtypeStruct((blocks // 2, tiles, cols), bf),
+        out_shape=jax.ShapeDtypeStruct((tiles, blocks // 2 * cols), bf),
         in_specs=[smem, smem] + [any_spec] * 8 + [vmem, vmem],
         out_specs=any_spec,
         scratch_shapes=[
@@ -544,12 +566,13 @@
             pltpu.VMEM((texts, width), bf),
             pltpu.VMEM((rows, feat), bf),
             pltpu.VMEM((rows, feat), bf),
-            pltpu.VMEM((TENANTS, feat, cols), bf),
-            pltpu.VMEM((TENANTS, feat, cols), bf),
-            pltpu.VMEM((2, blocks // 2, cols), jnp.float32),
-            pltpu.VMEM((TENANTS, rows, cols), bf),
-            pltpu.VMEM((2, rows, cols), bf),
-            pltpu.VMEM((2, rows, cols), bf),
+            pltpu.VMEM((TENANTS * cols, feat), bf),
+            pltpu.VMEM((TENANTS * cols, feat), bf),
+            pltpu.VMEM((2, 1, blocks // 2 * cols), jnp.float32),
+            pltpu.VMEM((rows, side), bf),
+            pltpu.VMEM((rows, side), bf),
+            pltpu.VMEM((rows, side), bf),
+            pltpu.VMEM((rows, side), bf),
             dma((6, heads_here, group - 1)),
             dma((6, heads_here, group - 1)),
             dma((6,)),
@@ -560,14 +583,14 @@
             dma,
             dma((2, heads_here, group - 1)),
             dma((2, heads_here, group - 1)),
-            dma((2,)),
-            dma((2,)),
-            dma((2, group)),
-            dma((blocks // 2,)),
-            dma((2,)),
+            dma((chunks,)),
+            dma((chunks,)),
+            dma((chunks, group)),
+            dma((group, chunks)),
+            dma((chunks,)),
         ],
         compiler_params=pltpu.CompilerParams(
-            collective_id=0, has_side_effects=True, vmem_limit_bytes=48 * 1024 * 1024
+            collective_id=0, has_side_effects=True, vmem_limit_bytes=60 * 1024 * 1024
         ),
         cost_estimate=pl.CostEstimate(
             flops=flops, bytes_accessed=16 * feat * cols, transcendentals=rows * heads_here * (padded + texts)
@@ -582,12 +605,11 @@
         cross_query,
         text_key,
         text_value,
-        wo_self,
-        wo_cross,
-        gate,
+        wo_self.T,
+        wo_cross.T,
+        attn_gate,
         mix,
     )
-    velocity = moved.transpose(1, 0, 2).reshape(tiles, blocks // 2 * cols)
     step = jnp.sum(jnp.where(jnp.arange(TENANTS) == tenant, t_index, 0))
     frac = 1.0 - step.astype(jnp.float32) / STEPS
     sigma = 5.0 * frac / (1.0 + 4.0 * frac)

time: 156 us -> 146 us (0.936)
  local copies, waits for them, and re-layouts: 9.33 us -> 2.13 us
  Pallas kernels: 141 us -> 139 us
    unnamed x24 -> x5, local copies, waits for them, and re-layouts: 7.81 us -> 0.82 us
    pallas_call x1, Pallas kernels: 141 us -> 139 us  [by_heads(): pl.pallas_call(functools.partial(fused_kernel, group), out_shape=jax.Shap...]
where the time goes in v2:
time: 146 us
  Pallas kernels  139 us (95%)
  other arithmetic  3.57 us (2%)
  local copies, waits for them, and re-layouts  2.13 us (1%)
    pallas_call x1, Pallas kernels, by_heads(): pl.pallas_call(functools.partial(fused_kernel, group), out_shape=jax.Shap...  139 us

profile of v2, /device:TPU:0, one launch (start us, length us, event | category | flops | bytes accessed | tf_op | source)
XLA Modules:
  0.0 145.7 jit_solution(151819014574252251)
XLA Ops:
  0.6 1.3 fusion
  2.6 1.3 reshape.7.mix_ref
  3.9 0.0 copy-start.1
  4.0 138.6 %attend_project.1 = bf16[112,2560]{1,0:T(8,128)(2,1)} custom-call(s32[4]{0:T(128)} %len_ref.1, s32[4]{0:T(128)} %text_ref.1, bf16[112,1536]{1,0:T(8,128)(2,1)} %q_in.1, bf16[112,1536]{1,0:T(8,128)(2,1)} %k_in.1, bf16[112,1536]{1,0:T(8,128)(2,1)} %v_in.1, bf16[112,1536]{1,0:T(8,128)(2,1)} %cq_in.1, bf16[128,1536]{1,0:T(8,128)(2,1)} %tk_in.1, ...), custom_call_target="tpu_custom_call" | custom-call | flops 4227858432 | bytes 7864320 | tf_op jit(solution)/shard_map/attend_project/pallas_call | solution.py:555
  142.6 0.0 copy-done.1
  142.6 0.0 copy-start
  142.6 2.3 %multiply_add_fusion = f32[112,2560]{1,0:T(8,128)} fusion(bf16[112,2560]{1,0:T(8,128)(2,1)} %attend_project.1, bf16[112,2560]{1,0:T(8,128)(2,1)S(1)} %copy-done.1, f32[]{:T(128)S(6)} %div.7), kind=kLoop, calls=%fused_computation | loop fusion | flops 1146880 | bytes 2293764 | tf_op jit(solution)/shard_map/add | solution.py:616
  144.9 0.0 copy-done
  144.9 0.8 copy.17
Async XLA Ops:
  3.9 138.6 %copy-start.1 = (bf16[112,2560]{1,0:T(8,128)(2,1)S(1)}, bf16[112,2560]{1,0:T(8,128)(2,1)}, u32[]{:S(2)}) copy-start(bf16[112,2560]{1,0:T(8,128)(2,1)} %param.24) | copy-start | bytes 1720324
  142.6 2.3 %copy-start = (bf16[112,2560]{1,0:T(8,128)(2,1)S(1)}, bf16[112,2560]{1,0:T(8,128)(2,1)}, u32[]{:S(2)}) copy-start(bf16[112,2560]{1,0:T(8,128)(2,1)} %attend_project.1) | copy-start | bytes 1720324

commit v3 on v2

--- a/solution.py
+++ b/solution.py
@@ -317,16 +317,45 @@
 
     gathered = [so_all, co_all]
 
-    def at_copy(i, h, k):
-        column = pl.ds(pl.multiple_of((z * heads_here + h) * DH, DH), DH)
+    def at_copy(i, h, source, way):
+        column = pl.ds(pl.multiple_of((source * heads_here + h) * DH, DH), DH)
         return pltpu.make_async_remote_copy(
             src_ref=gathered[i].at[:, column],
             dst_ref=gathered[i].at[:, column],
-            send_sem=at_send.at[i, h, k - 1],
-            recv_sem=at_recv.at[i, h, k - 1],
-            device_id=(peer(k) * TENANTS + t, y),
+            send_sem=at_send.at[i, h, source, way],
+            recv_sem=at_recv.at[i, h, source],
+            device_id=((z + 1 - 2 * way) * TENANTS + t, y),
             device_id_type=MESH,
         )
+
+    def both_ways(i, h, d, act):
+        for way in range(2):
+            source = z - d if way == 0 else z + d
+            onward = z < group - 1 if way == 0 else z > 0
+            here = source >= 0 if way == 0 else source < group
+
+            @pl.when(here)
+            def _():
+                act(at_copy(i, h, source, way), onward)
+
+    def relay(i, h, d):
+        def act(copy, onward):
+            if d > 0:
+                copy.wait_recv()
+
+            @pl.when(onward)
+            def _():
+                copy.start()
+
+        both_ways(i, h, d, act)
+
+    def settle(i, h, d):
+        def act(copy, onward):
+            @pl.when(onward)
+            def _():
+                copy.wait_send()
+
+        both_ways(i, h, d, act)
 
     def do_head(h, carry):
         here = pl.ds(pl.multiple_of(h * DH, DH), DH)
@@ -343,8 +372,15 @@
                 send_half(h + 1, i)
 
             gathered[i][:, column] = attend_head(qr[:, here], kr[:, here], vr[:, here], count)
-            for k in range(1, group):
-                at_copy(i, h, k).start()
+            relay(i, h, 0)
+            for d in range(1, group):
+                back = i - d
+                older = h + back // 2
+
+                @pl.when(older >= 0)
+                def _():
+                    relay(back % 2, older, d)
+
         return carry
 
     lax.fori_loop(0, heads_here, do_head, 0)
@@ -352,20 +388,17 @@
     for i in range(2):
         w_copy(i, 0).wait_recv()
         w_copy(i, 2).start()
+    pieces = 2 * heads_here
+    for step in range(pieces, pieces + group - 1):
+        for d in range(1, group):
+            if step - d < pieces:
+                relay((step - d) % 2, (step - d) // 2, d)
     for i in range(2):
         w_own(i).wait()
         w_copy(i, 1).wait_recv()
     for i in range(2):
         w_copy(i, 2).wait_recv()
     mix_copy.wait_recv()
-
-    def wait_attended(h, carry):
-        for i in range(2):
-            for k in range(1, group):
-                at_copy(i, h, k).wait_recv()
-        return carry
-
-    lax.fori_loop(0, heads_here, wait_attended, 0)
 
     side = term.shape[1]
     chunks = [(at, min(256, side - at)) for at in range(0, side, 256)]
@@ -456,8 +489,9 @@
         for k in range(1, group):
             for a in range(6):
                 in_copy(a, h, k).wait_send()
-            for i in range(2):
-                at_copy(i, h, k).wait_send()
+        for i in range(2):
+            for d in range(group - 1):
+                settle(i, h, d)
         return carry
 
     lax.fori_loop(0, heads_here, drain_head, 0)
@@ -581,8 +615,8 @@
             dma((2,)),
             dma,
             dma,
-            dma((2, heads_here, group - 1)),
-            dma((2, heads_here, group - 1)),
+            dma((2, heads_here, group, 2)),
+            dma((2, heads_here, group)),
             dma((chunks,)),
             dma((chunks,)),
             dma((chunks, group)),

time: 146 us -> 125 us (0.86)
  the two profiles are of different devices: /device:TPU:0 before, /device:TPU:6 now
where the time goes in v3:
time: 125 us
  Pallas kernels  117 us (94%)
  other arithmetic  3.57 us (3%)
  local copies, waits for them, and re-layouts  2.13 us (2%)
  between operations  1.37 us (1%)
    pallas_call x1, Pallas kernels, by_heads(): pl.pallas_call(functools.partial(fused_kernel, group), out_shape=jax.Shap...  117 us

profile of v3, /device:TPU:6, one launch (start us, length us, event | category | flops | bytes accessed | tf_op | source)
XLA Modules:
  0.0 124.5 jit_solution(8512430984874332672)
XLA Ops:
  0.6 1.3 %fusion = s32[]{:T(128)} fusion(s32[4]{0:T(128)} %param.27, s32[]{:T(128)S(6)} %select_n.11), kind=kLoop, calls=%fused_computation.2 | loop fusion | flops 11 | bytes 24 | tf_op jit(solution)/shard_map/reduce_sum | solution.py:647
  2.6 1.3 %reshape.7.mix_ref = f32[1,2560]{1,0:T(1,128)} reshape(f32[2560]{0:T(1024)} %param.23) | data formatting | bytes 20480 | tf_op jit(solution)/shard_map/reshape | solution.py:582
  3.9 0.0 copy-start.1
  4.0 117.4 %attend_project.1 = bf16[112,2560]{1,0:T(8,128)(2,1)} custom-call(s32[4]{0:T(128)} %len_ref.1, s32[4]{0:T(128)} %text_ref.1, bf16[112,1536]{1,0:T(8,128)(2,1)} %q_in.1, bf16[112,1536]{1,0:T(8,128)(2,1)} %k_in.1, bf16[112,1536]{1,0:T(8,128)(2,1)} %v_in.1, bf16[112,1536]{1,0:T(8,128)(2,1)} %cq_in.1, bf16[128,1536]{1,0:T(8,128)(2,1)} %tk_in.1, ...), custom_call_target="tpu_custom_call" | custom-call | flops 4227858432 | bytes 7864320 | tf_op jit(solution)/shard_map/attend_project/pallas_call | solution.py:589
  121.4 0.0 copy-done.1
  121.4 0.0 copy-start
  121.4 2.3 %multiply_add_fusion = f32[112,2560]{1,0:T(8,128)} fusion(bf16[112,2560]{1,0:T(8,128)(2,1)} %attend_project.1, bf16[112,2560]{1,0:T(8,128)(2,1)S(1)} %copy-done.1, f32[]{:T(128)S(6)} %div.7), kind=kLoop, calls=%fused_computation | loop fusion | flops 1146880 | bytes 2293764 | tf_op jit(solution)/shard_map/add | solution.py:650
  123.7 0.0 copy-done
  123.7 0.8 copy.17
Async XLA Ops:
  3.9 117.5 %copy-start.1 = (bf16[112,2560]{1,0:T(8,128)(2,1)S(1)}, bf16[112,2560]{1,0:T(8,128)(2,1)}, u32[]{:S(2)}) copy-start(bf16[112,2560]{1,0:T(8,128)(2,1)} %param.24) | copy-start | bytes 1720324
  121.4 2.3 %copy-start = (bf16[112,2560]{1,0:T(8,128)(2,1)S(1)}, bf16[112,2560]{1,0:T(8,128)(2,1)}, u32[]{:S(2)}) copy-start(bf16[112,2560]{1,0:T(8,128)(2,1)} %attend_project.1) | copy-start | bytes 1720324

commit v4 on v3

--- a/solution.py
+++ b/solution.py
@@ -152,6 +152,7 @@
     group,
     len_ref,
     text_ref,
+    step_ref,
     q_in,
     k_in,
     v_in,
@@ -163,6 +164,7 @@
     gate_ref,
     mix_ref,
     out,
+    sigma_ref,
     q_all,
     k_all,
     v_all,
@@ -174,6 +176,7 @@
     ws_all,
     wc_all,
     mix_all,
+    acc,
     term,
     term_own,
     term_in,
@@ -184,6 +187,7 @@
     w_send,
     w_recv,
     w_local,
+    mix_local,
     mix_send,
     mix_recv,
     at_send,
@@ -293,7 +297,10 @@
         own_copy(a).start()
     for i in range(2):
         w_own(i).start()
-    mix_all[y] = mix_ref[...]
+    mix_own = pltpu.make_async_copy(mix_ref, mix_all.at[y], mix_local)
+    mix_own.start()
+    frac = 1.0 - jnp.full(sigma_ref.shape, step_ref[t], jnp.int32).astype(jnp.float32) / STEPS
+    sigma_ref[...] = 5.0 * frac / (1.0 + 4.0 * frac)
     for ref, filled in ((k_all, rows), (v_all, rows), (tk_all, group * tk_in.shape[0]), (tv_all, group * tv_in.shape[0])):
         if ref.shape[0] > filled:
             ref[filled:, :] = jnp.zeros((ref.shape[0] - filled, ref.shape[1]), ref.dtype)
@@ -311,6 +318,7 @@
         w_copy(i, 0).start()
     for i in range(2):
         w_copy(i, 1).start()
+    mix_own.wait()
     mix_copy.start()
     for a in range(6):
         own_copy(a).wait()
@@ -367,6 +375,11 @@
                 for k in range(1, group):
                     in_copy(a, h, k).wait_recv()
 
+            @pl.when(h == heads_here - 1)
+            def _():
+                w_copy(i, 0).wait_recv()
+                w_copy(i, 2).start()
+
             @pl.when(h + 1 < heads_here)
             def _():
                 send_half(h + 1, i)
@@ -385,23 +398,10 @@
 
     lax.fori_loop(0, heads_here, do_head, 0)
 
-    for i in range(2):
-        w_copy(i, 0).wait_recv()
-        w_copy(i, 2).start()
-    pieces = 2 * heads_here
-    for step in range(pieces, pieces + group - 1):
-        for d in range(1, group):
-            if step - d < pieces:
-                relay((step - d) % 2, (step - d) // 2, d)
-    for i in range(2):
-        w_own(i).wait()
-        w_copy(i, 1).wait_recv()
-    for i in range(2):
-        w_copy(i, 2).wait_recv()
-    mix_copy.wait_recv()
-
     side = term.shape[1]
-    chunks = [(at, min(256, side - at)) for at in range(0, side, 256)]
+    lead = side % 256
+    chunks = [(0, lead)] if lead else []
+    chunks += [(at, 256) for at in range(lead, side, 256)]
 
     def term_copy(j):
         at, n = chunks[j]
@@ -414,27 +414,68 @@
             device_id_type=MESH,
         )
 
-    def project(whose, j):
+    def part(h, whose, j):
         at, n = chunks[j]
+        places = [slice((s * heads_here + h) * DH, (s * heads_here + h + 1) * DH) for s in range(group)]
         start = pl.multiple_of(whose * side + at, 128)
-        across_rows = (((1,), (1,)), ((), ()))
-        total = lax.dot_general(
-            so_all[...], ws_all[pl.ds(start, n), :], across_rows, preferred_element_type=jnp.float32
-        )
         first = pl.multiple_of(z * (2 * side) + whose * side + at, 128)
         gates = gate_ref[:, pl.ds(first, n)]
         mine = lax.broadcasted_iota(jnp.int32, gates.shape, 0) == t
-        total = jnp.sum(jnp.where(mine, gates, 0.0), axis=0, keepdims=True) * total
-        total = total + lax.dot_general(
-            co_all[...], wc_all[pl.ds(start, n), :], across_rows, preferred_element_type=jnp.float32
-        )
+        gates = jnp.sum(jnp.where(mine, gates, 0.0), axis=0, keepdims=True)
+
+        def product(left, right):
+            return lax.dot_general(
+                jnp.concatenate([left[:, p] for p in places], axis=1),
+                jnp.concatenate([right[pl.ds(start, n), p] for p in places], axis=1),
+                (((1,), (1,)), ((), ())),
+                preferred_element_type=jnp.float32,
+            )
+
+        return gates * product(so_all, ws_all) + product(co_all, wc_all)
+
+    def sums(whose, j):
+        at, n = chunks[j]
+        return (slice(None), pl.ds(pl.multiple_of(whose * side + at, 128), n))
+
+    def add_head(h):
+        for whose in (other, y):
+            for j in range(len(chunks)):
+                total = part(h, whose, j)
+                if h > 0:
+                    total = acc[sums(whose, j)] + total
+                acc[sums(whose, j)] = total
+
+    def last_head(whose, j):
+        total = part(heads_here - 1, whose, j)
+        if heads_here > 1:
+            total = acc[sums(whose, j)] + total
         return total.astype(jnp.bfloat16)
 
+    pieces = 2 * heads_here
+    added = 0
+    for step in range(pieces, pieces + group - 1):
+        for d in range(1, group):
+            if step - d < pieces:
+                relay((step - d) % 2, (step - d) // 2, d)
+        if step == pieces:
+            for i in range(2):
+                w_own(i).wait()
+                w_copy(i, 1).wait_recv()
+            for i in range(2):
+                w_copy(i, 2).wait_recv()
+        if added < heads_here - 1 and 2 * added + group <= step:
+            add_head(added)
+            added += 1
+    mix_copy.wait_recv()
+    while added < heads_here - 1:
+        add_head(added)
+        added += 1
+
     for j, (at, n) in enumerate(chunks):
-        term[:, at : at + n] = project(other, j)
+        term[:, at : at + n] = last_head(other, j)
         term_copy(j).start()
     for j, (at, n) in enumerate(chunks):
-        term_own[:, at : at + n] = project(y, j)
+        term_own[:, at : at + n] = last_head(y, j)
 
     source = lax.rem(z, half) * 2 + y
 
@@ -471,7 +512,8 @@
         branch = jnp.where(index < my_len, branch, 0.0)
         before = jnp.where(index == 0, 0.0, pltpu.roll(branch, 1, 0))
         after = jnp.where(index == rows - 1, 0.0, pltpu.roll(branch, rows - 1, 0))
-        mix = mix_all[y_out, :, out_columns(source, j)]
+        line = (source * side + at) // DH
+        mix = jnp.concatenate([mix_all[y_out, pl.ds(line + m, 1), :] for m in range(n // DH)], axis=1)
         speed = branch + mix * (before + after - 2.0 * branch)
         vel[:, at : at + n] = jnp.where(index < my_len, speed, 0.0).astype(jnp.bfloat16)
         for k in range(group - 1, 0, -1):
@@ -574,23 +616,23 @@
     rows = tiles * group
     padded = -(-rows // 128) * 128
     texts = -(-text_rows * group // 128) * 128
-    place = lax.axis_index("req")
-    tenant = place % TENANTS
-    slot = place // TENANTS
     side = cols * TENANTS // 2
     chunks = -(-side // 256)
-    mix = mix_coef.reshape(1, -1)
+    mix = mix_coef.reshape(-1, DH)
     bf = jnp.bfloat16
     dma = pltpu.SemaphoreType.DMA
     any_spec = pl.BlockSpec(memory_space=pltpu.HBM)
     smem = pl.BlockSpec(memory_space=pltpu.SMEM)
     vmem = pl.BlockSpec(memory_space=pltpu.VMEM)
     flops = 4 * rows * width * (padded + texts) + 4 * rows * feat * TENANTS * cols
-    velocity = pl.pallas_call(
+    velocity, sigma = pl.pallas_call(
         functools.partial(fused_kernel, group),
-        out_shape=jax.ShapeDtypeStruct((tiles, blocks // 2 * cols), bf),
-        in_specs=[smem, smem] + [any_spec] * 8 + [vmem, vmem],
-        out_specs=any_spec,
+        out_shape=(
+            jax.ShapeDtypeStruct((tiles, blocks // 2 * cols), bf),
+            jax.ShapeDtypeStruct((1, 128), jnp.float32),
+        ),
+        in_specs=[smem] * 3 + [any_spec] * 8 + [vmem, any_spec],
+        out_specs=(any_spec, vmem),
         scratch_shapes=[
             pltpu.VMEM((rows, width), bf),
             pltpu.VMEM((padded, width), bf),
@@ -602,7 +644,8 @@
             pltpu.VMEM((rows, feat), bf),
             pltpu.VMEM((TENANTS * cols, feat), bf),
             pltpu.VMEM((TENANTS * cols, feat), bf),
-            pltpu.VMEM((2, 1, blocks // 2 * cols), jnp.float32),
+            pltpu.VMEM((2, blocks // 2 * cols // DH, DH), jnp.float32),
+            pltpu.VMEM((rows, 2 * side), jnp.float32),
             pltpu.VMEM((rows, side), bf),
             pltpu.VMEM((rows, side), bf),
             pltpu.VMEM((rows, side), bf),
@@ -613,6 +656,7 @@
             dma((2, 3)),
             dma((2, 3)),
             dma((2,)),
+            dma,
             dma,
             dma,
             dma((2, heads_here, group, 2)),
@@ -633,6 +677,7 @@
     )(
         tenant_len,
         text_len,
+        t_index,
         query,
         key,
         value,
@@ -644,10 +689,7 @@
         attn_gate,
         mix,
     )
-    step = jnp.sum(jnp.where(jnp.arange(TENANTS) == tenant, t_index, 0))
-    frac = 1.0 - step.astype(jnp.float32) / STEPS
-    sigma = 5.0 * frac / (1.0 + 4.0 * frac)
-    return (velocity, latent.astype(jnp.float32) + sigma * velocity.astype(jnp.float32))
+    return (velocity, latent.astype(jnp.float32) + sigma[0, 0] * velocity.astype(jnp.float32))
 
 
 def either(*arrays):

time: 125 us -> 122 us (0.976)
  the two profiles are of different devices: /device:TPU:6 before, /device:TPU:0 now
where the time goes in v4:
time: 122 us; the launch traced here: 120 us
  Pallas kernels  116 us (95%)
  other arithmetic  2.95 us (2%)
    pallas_call x1, Pallas kernels, by_heads(): pl.pallas_call(functools.partial(fused_kernel, group), out_shape=(jax.Sha...  116 us
    add x1, other arithmetic, by_heads(): latent.astype(jnp.float32) + sigma[0, 0] * velocity.astype(jnp.float32)  2.95 us

profile of v4, /device:TPU:0, one launch (start us, length us, event | category | flops | bytes accessed | tf_op | source)
XLA Modules:
  0.0 120.5 jit_solution(9634139051522570025)
XLA Ops:
  0.6 0.0 copy-start.1
  0.6 116.0 %attend_project.1 = (bf16[112,2560]{1,0:T(8,128)(2,1)}, f32[1,128]{1,0:T(1,128)}) custom-call(s32[4]{0:T(128)} %len_ref.1, s32[4]{0:T(128)} %text_ref.1, s32[4]{0:T(128)} %step_ref.1, bf16[112,1536]{1,0:T(8,128)(2,1)} %q_in.1, bf16[112,1536]{1,0:T(8,128)(2,1)} %k_in.1, bf16[112,1536]{1,0:T(8,128)(2,1)} %v_in.1, bf16[112,1536]{1,0:T(8,128)(2,1)} %cq_in.1, ...), custom_call_target="tpu_custom_call" | custom-call | flops 4227858432 | bytes 7864320 | tf_op jit(solution)/shard_map/attend_project/pallas_call | solution.py:628
  116.7 0.0 copy-done.1
  116.7 0.0 copy-start
  116.7 2.9 %multiply_add_fusion = f32[112,2560]{1,0:T(8,128)} fusion(bf16[112,2560]{1,0:T(8,128)(2,1)} %get-tuple-element.8, bf16[112,2560]{1,0:T(8,128)(2,1)S(1)} %copy-done.1, f32[]{:T(128)} %bitcast.5), kind=kLoop, calls=%fused_computation | loop fusion | flops 1146880 | bytes 2293764 | tf_op jit(solution)/shard_map/add | solution.py:692
  119.7 0.0 copy-done
  119.7 0.8 copy.17
Async XLA Ops:
  0.6 116.1 %copy-start.1 = (bf16[112,2560]{1,0:T(8,128)(2,1)S(1)}, bf16[112,2560]{1,0:T(8,128)(2,1)}, u32[]{:S(2)}) copy-start(bf16[112,2560]{1,0:T(8,128)(2,1)} %param.24) | copy-start | bytes 1720324
  116.7 3.0 %copy-start = (bf16[112,2560]{1,0:T(8,128)(2,1)S(1)}, bf16[112,2560]{1,0:T(8,128)(2,1)}, u32[]{:S(2)}) copy-start(bf16[112,2560]{1,0:T(8,128)(2,1)} %get-tuple-element.8) | copy-start | bytes 1720324

commit v5 on v4

--- a/solution.py
+++ b/solution.py
@@ -176,7 +176,6 @@
     ws_all,
     wc_all,
     mix_all,
-    acc,
     term,
     term_own,
     term_in,
@@ -312,10 +311,14 @@
             for k in range(group - 1, 0, -1):
                 in_copy(a, h, k).start()
 
+    ahead = min(2, heads_here)
     send_half(0, 0)
     send_half(0, 1)
     for i in range(2):
         w_copy(i, 0).start()
+    for h in range(1, ahead):
+        send_half(h, 0)
+        send_half(h, 1)
     for i in range(2):
         w_copy(i, 1).start()
     mix_own.wait()
@@ -325,11 +328,19 @@
 
     gathered = [so_all, co_all]
 
+    window = half * tiles + 16
+    spans = [(0, window), (window, rows - window)]
+    late = heads_here
+
     def at_copy(i, h, source, way):
-        column = pl.ds(pl.multiple_of((source * heads_here + h) * DH, DH), DH)
+        width = DH
+        head, span = h, spans[0]
+        if isinstance(h, int) and h == late:
+            head, span, width = 0, spans[1], heads_here * DH
+        column = pl.ds(pl.multiple_of((source * heads_here + head) * DH, DH), width)
         return pltpu.make_async_remote_copy(
-            src_ref=gathered[i].at[:, column],
-            dst_ref=gathered[i].at[:, column],
+            src_ref=gathered[i].at[pl.ds(*span), column],
+            dst_ref=gathered[i].at[pl.ds(*span), column],
             send_sem=at_send.at[i, h, source, way],
             recv_sem=at_recv.at[i, h, source],
             device_id=((z + 1 - 2 * way) * TENANTS + t, y),
@@ -380,9 +391,9 @@
                 w_copy(i, 0).wait_recv()
                 w_copy(i, 2).start()
 
-            @pl.when(h + 1 < heads_here)
+            @pl.when(h + ahead < heads_here)
             def _():
-                send_half(h + 1, i)
+                send_half(h + ahead, i)
 
             gathered[i][:, column] = attend_head(qr[:, here], kr[:, here], vr[:, here], count)
             relay(i, h, 0)
@@ -403,20 +414,21 @@
     chunks = [(0, lead)] if lead else []
     chunks += [(at, 256) for at in range(lead, side, 256)]
 
-    def term_copy(j):
+    def term_copy(part, j):
         at, n = chunks[j]
+        where = (pl.ds(*spans[part]), pl.ds(at, n))
         return pltpu.make_async_remote_copy(
-            src_ref=term.at[:, pl.ds(at, n)],
-            dst_ref=term_in.at[:, pl.ds(at, n)],
-            send_sem=term_send.at[j],
-            recv_sem=term_recv.at[j],
+            src_ref=term.at[where],
+            dst_ref=term_in.at[where],
+            send_sem=term_send.at[part, j],
+            recv_sem=term_recv.at[part, j],
             device_id=(place, other),
             device_id_type=MESH,
         )
 
-    def part(h, whose, j):
+    def project(part, whose, j):
         at, n = chunks[j]
-        places = [slice((s * heads_here + h) * DH, (s * heads_here + h + 1) * DH) for s in range(group)]
+        lo, count = spans[part]
         start = pl.multiple_of(whose * side + at, 128)
         first = pl.multiple_of(z * (2 * side) + whose * side + at, 128)
         gates = gate_ref[:, pl.ds(first, n)]
@@ -425,107 +437,120 @@
 
         def product(left, right):
             return lax.dot_general(
-                jnp.concatenate([left[:, p] for p in places], axis=1),
-                jnp.concatenate([right[pl.ds(start, n), p] for p in places], axis=1),
+                left[lo : lo + count, :],
+                right[pl.ds(start, n), :],
                 (((1,), (1,)), ((), ())),
                 preferred_element_type=jnp.float32,
             )
 
-        return gates * product(so_all, ws_all) + product(co_all, wc_all)
-
-    def sums(whose, j):
+        return (gates * product(so_all, ws_all) + product(co_all, wc_all)).astype(jnp.bfloat16)
+
+    source = lax.rem(z, half) * 2 + y
+
+    def out_columns(sender, j):
         at, n = chunks[j]
-        return (slice(None), pl.ds(pl.multiple_of(whose * side + at, 128), n))
-
-    def add_head(h):
-        for whose in (other, y):
-            for j in range(len(chunks)):
-                total = part(h, whose, j)
-                if h > 0:
-                    total = acc[sums(whose, j)] + total
-                acc[sums(whose, j)] = total
-
-    def last_head(whose, j):
-        total = part(heads_here - 1, whose, j)
-        if heads_here > 1:
-            total = acc[sums(whose, j)] + total
-        return total.astype(jnp.bfloat16)
+        return pl.ds(pl.multiple_of(sender * side + at, 128), n)
+
+    def vel_part(j, to):
+        at, n = chunks[j]
+        return vel.at[pl.ds(to * tiles, tiles), pl.ds(at, n)]
+
+    def out_copy(j, to):
+        return pltpu.make_async_remote_copy(
+            src_ref=vel_part(j, to),
+            dst_ref=out.at[:, out_columns(source, j)],
+            send_sem=out_send.at[j, to],
+            recv_sem=out_recv.at[source, j],
+            device_id=(to * TENANTS + t, y_out),
+            device_id_type=MESH,
+        )
+
+    def out_own(j, to):
+        return pltpu.make_async_copy(
+            vel_part(j, to), out.at[:, out_columns(source, j)], out_local.at[j]
+        )
+
+    def stays(to):
+        return jnp.logical_and(z == to, y_out == y)
+
+    def send_out(j, to):
+        @pl.when(stays(to))
+        def _():
+            out_own(j, to).start()
+
+        @pl.when(jnp.logical_not(stays(to)))
+        def _():
+            out_copy(j, to).start()
+
+    def finish_out(j, to):
+        @pl.when(stays(to))
+        def _():
+            out_own(j, to).wait()
+
+        @pl.when(jnp.logical_not(stays(to)))
+        def _():
+            out_copy(j, to).wait_send()
+
+    def swap(part):
+        lo, count = spans[part]
+        for j, (at, n) in enumerate(chunks):
+            term[lo : lo + count, at : at + n] = project(part, other, j)
+            term_copy(part, j).start()
+
+    def keep(part):
+        lo, count = spans[part]
+        for j, (at, n) in enumerate(chunks):
+            term_own[lo : lo + count, at : at + n] = project(part, y, j)
+
+    def smooth(part):
+        lo = part * (rows - window)
+        skip = part * 16
+        for j, (at, n) in enumerate(chunks):
+            term_copy(part, j).wait_recv()
+            total = term_own[lo : lo + window, at : at + n].astype(jnp.float32)
+            total = total + term_in[lo : lo + window, at : at + n].astype(jnp.float32)
+            branch = total.astype(jnp.bfloat16).astype(jnp.float32)
+            index = lo + lax.broadcasted_iota(jnp.int32, branch.shape, 0)
+            branch = jnp.where(index < my_len, branch, 0.0)
+            before = jnp.where(index == 0, 0.0, pltpu.roll(branch, 1, 0))
+            after = jnp.where(index == rows - 1, 0.0, pltpu.roll(branch, window - 1, 0))
+            line = (source * side + at) // DH
+            mix = jnp.concatenate(
+                [mix_all[y_out, pl.ds(line + m, 1), :] for m in range(n // DH)], axis=1
+            )
+            speed = branch + mix * (before + after - 2.0 * branch)
+            speed = jnp.where(index < my_len, speed, 0.0).astype(jnp.bfloat16)
+            vel[lo + skip : lo + skip + half * tiles, at : at + n] = speed[skip : skip + half * tiles]
+            for to in range(part * half, part * half + half):
+                send_out(j, to)
 
     pieces = 2 * heads_here
-    added = 0
+    for i in range(2):
+        relay(i, late, 0)
     for step in range(pieces, pieces + group - 1):
         for d in range(1, group):
             if step - d < pieces:
                 relay((step - d) % 2, (step - d) // 2, d)
-        if step == pieces:
-            for i in range(2):
-                w_own(i).wait()
-                w_copy(i, 1).wait_recv()
-            for i in range(2):
-                w_copy(i, 2).wait_recv()
-        if added < heads_here - 1 and 2 * added + group <= step:
-            add_head(added)
-            added += 1
+    for i in range(2):
+        w_own(i).wait()
+        w_copy(i, 1).wait_recv()
+    for i in range(2):
+        w_copy(i, 2).wait_recv()
     mix_copy.wait_recv()
-    while added < heads_here - 1:
-        add_head(added)
-        added += 1
-
-    for j, (at, n) in enumerate(chunks):
-        term[:, at : at + n] = last_head(other, j)
-        term_copy(j).start()
-    for j, (at, n) in enumerate(chunks):
-        term_own[:, at : at + n] = last_head(y, j)
-
-    source = lax.rem(z, half) * 2 + y
-
-    def out_columns(sender, j):
-        at, n = chunks[j]
-        return pl.ds(pl.multiple_of(sender * side + at, 128), n)
-
-    def vel_part(j, to):
-        at, n = chunks[j]
-        return vel.at[pl.ds(pl.multiple_of(to * tiles, 16), tiles), pl.ds(at, n)]
-
-    def out_copy(j, k):
-        to = peer(k)
-        return pltpu.make_async_remote_copy(
-            src_ref=vel_part(j, to),
-            dst_ref=out.at[:, out_columns(source, j)],
-            send_sem=out_send.at[j, k],
-            recv_sem=out_recv.at[source, j],
-            device_id=(to * TENANTS + t, y_out),
-            device_id_type=MESH,
-        )
-
-    def out_own(j):
-        return pltpu.make_async_copy(
-            vel_part(j, z), out.at[:, out_columns(source, j)], out_local.at[j]
-        )
-
-    for j, (at, n) in enumerate(chunks):
-        term_copy(j).wait_recv()
-        total = term_own[:, at : at + n].astype(jnp.float32)
-        total = total + term_in[:, at : at + n].astype(jnp.float32)
-        branch = total.astype(jnp.bfloat16).astype(jnp.float32)
-        index = lax.broadcasted_iota(jnp.int32, branch.shape, 0)
-        branch = jnp.where(index < my_len, branch, 0.0)
-        before = jnp.where(index == 0, 0.0, pltpu.roll(branch, 1, 0))
-        after = jnp.where(index == rows - 1, 0.0, pltpu.roll(branch, rows - 1, 0))
-        line = (source * side + at) // DH
-        mix = jnp.concatenate([mix_all[y_out, pl.ds(line + m, 1), :] for m in range(n // DH)], axis=1)
-        speed = branch + mix * (before + after - 2.0 * branch)
-        vel[:, at : at + n] = jnp.where(index < my_len, speed, 0.0).astype(jnp.bfloat16)
-        for k in range(group - 1, 0, -1):
-            out_copy(j, k).start()
-
-        @pl.when(y_out == y)
-        def _():
-            out_own(j).start()
-
-        @pl.when(y_out != y)
-        def _():
-            out_copy(j, 0).start()
+    stages = [lambda: swap(0), lambda: keep(0), lambda: smooth(0)]
+    for d in range(1, group):
+        for i in range(2):
+            relay(i, late, d)
+        if d < group - 1 and stages:
+            stages.pop(0)()
+        if d == group - 2:
+            while stages:
+                stages.pop(0)()
+    while stages:
+        stages.pop(0)()
+    swap(1)
+    keep(1)
+    smooth(1)
 
     def drain_head(h, carry):
         for k in range(1, group):
@@ -542,18 +567,14 @@
             w_copy(i, hop).wait_send()
     mix_copy.wait_send()
 
+    for i in range(2):
+        for d in range(group - 1):
+            settle(i, late, d)
     for j in range(len(chunks)):
-        term_copy(j).wait_send()
-        for k in range(1, group):
-            out_copy(j, k).wait_send()
-
-        @pl.when(y_out == y)
-        def _():
-            out_own(j).wait()
-
-        @pl.when(y_out != y)
-        def _():
-            out_copy(j, 0).wait_send()
+        for part in range(2):
+            term_copy(part, j).wait_send()
+        for to in range(group):
+            finish_out(j, to)
 
     def arrive(sender, carry):
         mine = jnp.logical_and(y_out == y, sender == source)
@@ -645,7 +666,6 @@
             pltpu.VMEM((TENANTS * cols, feat), bf),
             pltpu.VMEM((TENANTS * cols, feat), bf),
             pltpu.VMEM((2, blocks // 2 * cols // DH, DH), jnp.float32),
-            pltpu.VMEM((rows, 2 * side), jnp.float32),
             pltpu.VMEM((rows, side), bf),
             pltpu.VMEM((rows, side), bf),
             pltpu.VMEM((rows, side), bf),
@@ -659,10 +679,10 @@
             dma,
             dma,
             dma,
-            dma((2, heads_here, group, 2)),
-            dma((2, heads_here, group)),
-            dma((chunks,)),
-            dma((chunks,)),
+            dma((2, heads_here + 1, group, 2)),
+            dma((2, heads_here + 1, group)),
+            dma((2, chunks)),
+            dma((2, chunks)),
             dma((chunks, group)),
             dma((group, chunks)),
             dma((chunks,)),

time: 122 us -> 122 us (level)
  no operation moved by 1% of the time
where the time goes in v5:
time: 122 us; the launch traced here: 121 us
  Pallas kernels  117 us (96%)
  other arithmetic  2.95 us (2%)
    pallas_call x1, Pallas kernels, by_heads(): pl.pallas_call(functools.partial(fused_kernel, group), out_shape=(jax.Sha...  117 us
    add x1, other arithmetic, by_heads(): latent.astype(jnp.float32) + sigma[0, 0] * velocity.astype(jnp.float32)  2.95 us

profile of v5, /device:TPU:0, one launch (start us, length us, event | category | flops | bytes accessed | tf_op | source)
XLA Modules:
  0.0 121.4 jit_solution(16178426222030089729)
XLA Ops:
  0.6 0.0 copy-start.1
  0.6 117.0 %attend_project.1 = (bf16[112,2560]{1,0:T(8,128)(2,1)}, f32[1,128]{1,0:T(1,128)}) custom-call(s32[4]{0:T(128)} %len_ref.1, s32[4]{0:T(128)} %text_ref.1, s32[4]{0:T(128)} %step_ref.1, bf16[112,1536]{1,0:T(8,128)(2,1)} %q_in.1, bf16[112,1536]{1,0:T(8,128)(2,1)} %k_in.1, bf16[112,1536]{1,0:T(8,128)(2,1)} %v_in.1, bf16[112,1536]{1,0:T(8,128)(2,1)} %cq_in.1, ...), custom_call_target="tpu_custom_call" | custom-call | flops 4227858432 | bytes 7864320 | tf_op jit(solution)/shard_map/attend_project/pallas_call | solution.py:649
  117.7 0.0 copy-done.1
  117.7 0.0 copy-start
  117.7 2.9 %multiply_add_fusion = f32[112,2560]{1,0:T(8,128)} fusion(bf16[112,2560]{1,0:T(8,128)(2,1)} %get-tuple-element.8, bf16[112,2560]{1,0:T(8,128)(2,1)S(1)} %copy-done.1, f32[]{:T(128)} %bitcast.5), kind=kLoop, calls=%fused_computation | loop fusion | flops 1146880 | bytes 2293764 | tf_op jit(solution)/shard_map/add | solution.py:712
  120.6 0.0 copy-done
  120.6 0.8 copy.17
Async XLA Ops:
  0.6 117.0 %copy-start.1 = (bf16[112,2560]{1,0:T(8,128)(2,1)S(1)}, bf16[112,2560]{1,0:T(8,128)(2,1)}, u32[]{:S(2)}) copy-start(bf16[112,2560]{1,0:T(8,128)(2,1)} %param.24) | copy-start | bytes 1720324
  117.7 3.0 %copy-start = (bf16[112,2560]{1,0:T(8,128)(2,1)S(1)}, bf16[112,2560]{1,0:T(8,128)(2,1)}, u32[]{:S(2)}) copy-start(bf16[112,2560]{1,0:T(8,128)(2,1)} %get-tuple-element.8) | copy-start | bytes 1720324

commit v6 on v5

--- a/solution.py
+++ b/solution.py
@@ -267,18 +267,19 @@
         src, dst = weights[i]
         return pltpu.make_async_copy(src, dst.at[w_rows(t), :], w_local.at[i])
 
-    def w_copy(i, hop):
+    bounds = [cols // 16 * c // heads_here * 16 for c in range(heads_here + 1)]
+
+    def w_copy(i, hop, c):
         src, dst = weights[i]
-        if hop == 2:
-            src, block = dst.at[w_rows(across), :], across
-        else:
-            block = t
+        low, n = bounds[c], bounds[c + 1] - bounds[c]
+        block = across if hop == 2 else t
+        there = dst.at[pl.ds(pl.multiple_of(block * cols + low, 16), n), :]
         target = across if hop == 0 else sibling
         return pltpu.make_async_remote_copy(
-            src_ref=src,
-            dst_ref=dst.at[w_rows(block), :],
-            send_sem=w_send.at[i, hop],
-            recv_sem=w_recv.at[i, hop],
+            src_ref=there if hop == 2 else src.at[pl.ds(low, n), :],
+            dst_ref=there,
+            send_sem=w_send.at[i, hop, c],
+            recv_sem=w_recv.at[i, hop, c],
             device_id=(z * TENANTS + target, y),
             device_id_type=MESH,
         )
@@ -315,12 +316,10 @@
     send_half(0, 0)
     send_half(0, 1)
     for i in range(2):
-        w_copy(i, 0).start()
+        w_copy(i, 0, 0).start()
     for h in range(1, ahead):
         send_half(h, 0)
         send_half(h, 1)
-    for i in range(2):
-        w_copy(i, 1).start()
     mix_own.wait()
     mix_copy.start()
     for a in range(6):
@@ -386,17 +385,23 @@
                 for k in range(1, group):
                     in_copy(a, h, k).wait_recv()
 
-            @pl.when(h == heads_here - 1)
-            def _():
-                w_copy(i, 0).wait_recv()
-                w_copy(i, 2).start()
-
             @pl.when(h + ahead < heads_here)
             def _():
                 send_half(h + ahead, i)
 
             gathered[i][:, column] = attend_head(qr[:, here], kr[:, here], vr[:, here], count)
             relay(i, h, 0)
+            for c in range(heads_here):
+
+                @pl.when(h == c)
+                def _():
+                    if c + 1 < heads_here:
+                        w_copy(i, 0, c + 1).start()
+                    w_copy(i, 1, c).start()
+                    if c > 0:
+                        w_copy(i, 0, c - 1).wait_recv()
+                        w_copy(i, 2, c - 1).start()
+
             for d in range(1, group):
                 back = i - d
                 older = h + back // 2
@@ -527,15 +532,18 @@
     pieces = 2 * heads_here
     for i in range(2):
         relay(i, late, 0)
+    for i in range(2):
+        w_copy(i, 0, heads_here - 1).wait_recv()
+        w_copy(i, 2, heads_here - 1).start()
     for step in range(pieces, pieces + group - 1):
         for d in range(1, group):
             if step - d < pieces:
                 relay((step - d) % 2, (step - d) // 2, d)
     for i in range(2):
         w_own(i).wait()
-        w_copy(i, 1).wait_recv()
-    for i in range(2):
-        w_copy(i, 2).wait_recv()
+        for hop in (1, 2):
+            for c in range(heads_here):
+                w_copy(i, hop, c).wait_recv()
     mix_copy.wait_recv()
     stages = [lambda: swap(0), lambda: keep(0), lambda: smooth(0)]
     for d in range(1, group):
@@ -564,7 +572,8 @@
     lax.fori_loop(0, heads_here, drain_head, 0)
     for i in range(2):
         for hop in range(3):
-            w_copy(i, hop).wait_send()
+            for c in range(heads_here):
+                w_copy(i, hop, c).wait_send()
     mix_copy.wait_send()
 
     for i in range(2):
@@ -673,8 +682,8 @@
             dma((6, heads_here, group - 1)),
             dma((6, heads_here, group - 1)),
             dma((6,)),
-            dma((2, 3)),
-            dma((2, 3)),
+            dma((2, 3, heads_here)),
+            dma((2, 3, heads_here)),
             dma((2,)),
             dma,
             dma,

time: 122 us -> 122 us (level)
  no operation moved by 1% of the time
where the time goes in v6:
time: 122 us
  Pallas kernels  117 us (96%)
  other arithmetic  2.95 us (2%)
    pallas_call x1, Pallas kernels, by_heads(): pl.pallas_call(functools.partial(fused_kernel, group), out_shape=(jax.Sha...  117 us
    add x1, other arithmetic, by_heads(): latent.astype(jnp.float32) + sigma[0, 0] * velocity.astype(jnp.float32)  2.95 us

profile of v6, /device:TPU:0, one launch (start us, length us, event | category | flops | bytes accessed | tf_op | source)
XLA Modules:
  0.0 121.6 jit_solution(13400583351811131665)
XLA Ops:
  0.6 0.0 copy-start.1
  0.6 117.2 %attend_project.1 = (bf16[112,2560]{1,0:T(8,128)(2,1)}, f32[1,128]{1,0:T(1,128)}) custom-call(s32[4]{0:T(128)} %len_ref.1, s32[4]{0:T(128)} %text_ref.1, s32[4]{0:T(128)} %step_ref.1, bf16[112,1536]{1,0:T(8,128)(2,1)} %q_in.1, bf16[112,1536]{1,0:T(8,128)(2,1)} %k_in.1, bf16[112,1536]{1,0:T(8,128)(2,1)} %v_in.1, bf16[112,1536]{1,0:T(8,128)(2,1)} %cq_in.1, ...), custom_call_target="tpu_custom_call" | custom-call | flops 4227858432 | bytes 7864320 | tf_op jit(solution)/shard_map/attend_project/pallas_call | solution.py:658
  117.9 0.0 copy-done.1
  117.9 0.0 copy-start
  117.9 2.9 %multiply_add_fusion = f32[112,2560]{1,0:T(8,128)} fusion(bf16[112,2560]{1,0:T(8,128)(2,1)} %get-tuple-element.8, bf16[112,2560]{1,0:T(8,128)(2,1)S(1)} %copy-done.1, f32[]{:T(128)} %bitcast.5), kind=kLoop, calls=%fused_computation | loop fusion | flops 1146880 | bytes 2293764 | tf_op jit(solution)/shard_map/add | solution.py:721
  120.8 0.0 copy-done
  120.8 0.8 copy.17
Async XLA Ops:
  0.6 117.2 %copy-start.1 = (bf16[112,2560]{1,0:T(8,128)(2,1)S(1)}, bf16[112,2560]{1,0:T(8,128)(2,1)}, u32[]{:S(2)}) copy-start(bf16[112,2560]{1,0:T(8,128)(2,1)} %param.24) | copy-start | bytes 1720324
  117.9 3.0 %copy-start = (bf16[112,2560]{1,0:T(8,128)(2,1)S(1)}, bf16[112,2560]{1,0:T(8,128)(2,1)}, u32[]{:S(2)}) copy-start(bf16[112,2560]{1,0:T(8,128)(2,1)} %get-tuple-element.8) | copy-start | bytes 1720324
